TPU v7x, 32 devices: a whole 2x2x4 slice. The times are simulated.
32 devices in a mesh: seq: 16 (over z, y, core), head: 2 (over x).
Axes of the slice: x: 2, y: 2, z: 4, core: 2. Of those that a mesh axis runs over, the one named last changes fastest.
Arguments:
- queries: bfloat16 [16384, 4096], P('seq', 'head'), may hold values from -6 to 6
- keys: bfloat16 [16384, 4096], P('seq', 'head'), may hold values from -6 to 6
- values: bfloat16 [16384, 4096], P('seq', 'head'), may hold values from -6 to 6
- out_weight: bfloat16 [4096, 4096], P('head'), may hold values from -1.5 to 1.5
Outputs:
- mixed: bfloat16 [16384, 4096], P('seq', 'head')
All inputs are finite; a program needn't handle non-finite values.
Results may differ from a plain program's by a relative error of at most 0.015.
Values may be sent and summed in bfloat16 or wider, within the bound.
No kernel may reach another device: no remote copies, remote signals or barrier semaphores. Data moves between devices by JAX's collectives and lax.ppermute only.
A program may use at most 192 MiB of HBM per device.

v0:
```python
import math

import jax
import jax.numpy as jnp
from jax import lax
from jax.sharding import PartitionSpec as P

HEAD_DIM = 128
SEG1 = 2048
SEG2 = 8192


NEG_FILL = -1e30


def passed_along(value, axis, steps):
    count = lax.axis_size(axis)
    leading, last = (max(0, -steps), min(count, count - steps))
    return lax.ppermute(value, axis, [(source, source + steps) for source in range(leading, last)])


def attend_block(query, key_rows, value_rows, valid, scale):
    scores = jnp.einsum("qhd,khd->hqk", query, key_rows, preferred_element_type=jnp.float32) * scale
    scores = jnp.where(valid, scores, NEG_FILL)
    peak = jnp.max(scores, axis=-1)
    weights = jnp.where(valid, jnp.exp(scores - peak[..., None]), 0.0)
    total = jnp.sum(weights, axis=-1)
    numer = jnp.einsum(
        "hqk,khd->hqd", weights.astype(jnp.bfloat16), value_rows, preferred_element_type=jnp.float32
    )
    return (numer, peak, total)


def absorb_block(state, query, key_rows, value_rows, valid, scale):
    numer, peak, total = state
    scores = jnp.einsum("qhd,khd->hqk", query, key_rows, preferred_element_type=jnp.float32) * scale
    scores = jnp.where(valid, scores, NEG_FILL)
    new_peak = jnp.maximum(peak, jnp.max(scores, axis=-1))
    weights = jnp.where(valid, jnp.exp(scores - new_peak[..., None]), 0.0)
    added = jnp.einsum(
        "hqk,khd->hqd", weights.astype(jnp.bfloat16), value_rows, preferred_element_type=jnp.float32
    )
    return (added, new_peak, jnp.sum(weights, axis=-1))


def take_dilated(source, stride, offsets):
    count = source.shape[0] // stride
    shaped = source.reshape(count, stride, offsets.shape[0], -1)
    picker = (jnp.arange(stride)[:, None] == offsets[None, :]).astype(source.dtype)
    return jnp.sum(shaped * picker[None, :, :, None], axis=1).reshape(count, -1)


def spread_rows(state, stride, offsets):
    numer, peak, total = state
    heads_here, count = peak.shape
    picker = jnp.arange(stride)[None, :] == offsets[:, None]
    numer_full = jnp.where(picker[:, None, :, None], numer[:, :, None, :], 0.0).reshape(
        heads_here, count * stride, -1
    )
    peak_full = jnp.where(picker[:, None, :], peak[:, :, None], NEG_FILL).reshape(
        heads_here, count * stride
    )
    total_full = jnp.where(picker[:, None, :], total[:, :, None], 0.0).reshape(
        heads_here, count * stride
    )
    return (numer_full, peak_full, total_full)


def shards(queries, keys, values, out_weight):
    tok_rows = queries.shape[0]
    heads_here = queries.shape[1] // HEAD_DIM
    scale = 1.0 / math.sqrt(HEAD_DIM)
    seq_index = lax.axis_index("seq")
    head_index = lax.axis_index("head")
    head_ids = head_index * heads_here + jnp.arange(heads_here)
    query_pos = seq_index * tok_rows + jnp.arange(tok_rows)
    near_span = SEG1 // tok_rows
    near_keys, near_values = (keys, values)
    level_bit = 0
    moved = passed_along((near_keys, near_values), "seq", 1 << level_bit)
    near_keys = jnp.concatenate([moved[0], near_keys], axis=0)
    near_values = jnp.concatenate([moved[1], near_values], axis=0)
    near_pos = (seq_index - near_span + 1) * tok_rows + jnp.arange(near_span * tok_rows)
    near_start = seq_index // near_span * near_span * tok_rows
    near_valid = (near_pos[None, :] <= query_pos[:, None]) & (near_pos[None, :] >= near_start)

    def near_head(head_slot):
        column = head_slot * HEAD_DIM
        query = lax.dynamic_slice_in_dim(queries, column, HEAD_DIM, 1)[:, None, :]
        key_rows = lax.dynamic_slice_in_dim(near_keys, column, HEAD_DIM, 1)[:, None, :]
        value_rows = lax.dynamic_slice_in_dim(near_values, column, HEAD_DIM, 1)[:, None, :]
        numer, peak, total = attend_block(query, key_rows, value_rows, near_valid[None], scale)
        return (numer[0], peak[0], total[0])

    near_state = lax.map(near_head, jnp.arange(heads_here))
    mid_offsets = head_ids % 4
    far_offsets = head_ids % 16
    mid_count = tok_rows // 4
    far_count = tok_rows // 16
    mid_query = take_dilated(queries, 4, mid_offsets).reshape(mid_count, heads_here, HEAD_DIM)
    far_query = take_dilated(queries, 16, far_offsets).reshape(far_count, heads_here, HEAD_DIM)
    mid_keys = take_dilated(keys, 4, mid_offsets)
    mid_values = take_dilated(values, 4, mid_offsets)
    mid_qpos = seq_index * tok_rows + mid_offsets[:, None] + 4 * jnp.arange(mid_count)[None, :]
    far_qpos = seq_index * tok_rows + far_offsets[:, None] + 16 * jnp.arange(far_count)[None, :]
    mid_span = SEG2 // tok_rows
    mid_start = seq_index // mid_span * mid_span * tok_rows
    empty_far = (
        jnp.zeros((heads_here, far_count, HEAD_DIM), jnp.float32),
        jnp.full((heads_here, far_count), NEG_FILL, jnp.float32),
        jnp.zeros((heads_here, far_count), jnp.float32),
    )
    block_keys, block_values = (mid_keys, mid_values)
    for level_bit in range(mid_span.bit_length() - 1):
        moved = passed_along((block_keys, block_values), "seq", 1 << level_bit)
        block_keys = jnp.concatenate([moved[0], block_keys], axis=0)
        block_values = jnp.concatenate([moved[1], block_values], axis=0)
    key_index = jnp.arange(mid_span * mid_count)
    mid_kpos = (
        (seq_index - mid_span + 1) * tok_rows
        + (key_index // mid_count * tok_rows + 4 * (key_index % mid_count))[None, :]
        + mid_offsets[:, None]
    )
    mid_valid = (mid_kpos[:, None, :] <= mid_qpos[:, :, None]) & (mid_kpos[:, None, :] >= mid_start)
    mid_state = attend_block(
        mid_query,
        block_keys.reshape(-1, heads_here, HEAD_DIM),
        block_values.reshape(-1, heads_here, HEAD_DIM),
        mid_valid,
        scale,
    )
    far_keys = take_dilated(keys, 16, far_offsets)
    far_values = take_dilated(values, 16, far_offsets)
    piece = (
        lax.all_gather(far_keys, "seq", axis=0, tiled=True),
        lax.all_gather(far_values, "seq", axis=0, tiled=True),
    )
    count = piece[0].shape[0]
    row_index = jnp.arange(count)
    key_pos = (row_index // far_count * tok_rows + 16 * (row_index % far_count))[
        None, :
    ] + far_offsets[:, None]
    valid = key_pos[:, None, :] <= far_qpos[:, :, None]
    far_state = absorb_block(
        empty_far,
        far_query,
        piece[0].reshape(count, heads_here, HEAD_DIM),
        piece[1].reshape(count, heads_here, HEAD_DIM),
        valid,
        scale,
    )
    levels = (
        near_state,
        spread_rows(mid_state, 4, mid_offsets),
        spread_rows(far_state, 16, far_offsets),
    )
    top = jnp.maximum(jnp.maximum(levels[0][1], levels[1][1]), levels[2][1])
    numer = jnp.zeros_like(levels[0][0])
    total = jnp.zeros_like(levels[0][2])
    for level in levels:
        factor = jnp.exp(level[1] - top)
        numer = numer + level[0] * factor[..., None]
        total = total + level[2] * factor
    attended = (
        jnp.transpose(numer / total[..., None], (1, 0, 2))
        .reshape(tok_rows, -1)
        .astype(jnp.bfloat16)
    )
    terms = jnp.dot(attended, out_weight, preferred_element_type=jnp.float32)
    return lax.psum_scatter(terms.astype(jnp.bfloat16), "head", scatter_dimension=1, tiled=True)


def solution(mesh):
    placed = (P("seq", "head"), P("seq", "head"), P("seq", "head"), P("head", None))
    return jax.shard_map(
        shards, mesh=mesh, in_specs=placed, out_specs=P("seq", "head"), check_vma=False
    )
```

profile of v0, /device:TPU:1, one launch (start us, length us, event | category | flops | bytes accessed | tf_op | source)
XLA Modules:
  0.0 1051.3 jit_solution(3518470247712972704)
XLA Ops:
  13.3 6.5 fusion.39
  25.2 10.7 %multiply_reduce_fusion = (bf16[256,16,128]{2,1,0:T(8,128)(2,1)S(1)}, bf16[256,16,128]{2,1,0:T(8,128)(2,1)S(1)}, bf16[256,16,128]{2,1,0:T(8,128)(2,1)}) fusion(bf16[256,4,16,128]{3,2,1,0:T(8,128)(2,1)} %bitcast.91, bf16[4,16]{1,0:T(4,128)(2,1)S(1)} %fusion.76, bf16[256,4,16,128]{3,2,1,0:T(8,128)(2,1)} %bitcast.89, bf16[256,4,16,128]{3,2,1,0:T(8,128)(2,1)} %bitcast.87), kind=kLoop, calls=%fused_computation.57 | loop fusion | flops 11010048 | bytes 15728768 | tf_op jit(solution)/shard_map/reduce_sum | solution.py:50
  46.7 52.3 %collective-permute-done.2 = bf16[256,2048]{0,1:T(8,128)(2,1)} collective-permute-done((bf16[256,2048]{0,1:T(8,128)(2,1)}, bf16[256,2048]{0,1:T(8,128)(2,1)}, u32[]{:S(2)}, u32[]{:S(2)}) %collective-permute-start.2) | collective-permute-done | bytes 1048608 | tf_op jit(solution)/shard_map/ppermute | solution.py:19
  102.0 30.0 %collective-permute-start.3 = (bf16[512,2048]{0,1:T(8,128)(2,1)}, bf16[512,2048]{0,1:T(8,128)(2,1)}, u32[]{:S(2)}, u32[]{:S(2)}) collective-permute-start(bf16[512,2048]{0,1:T(8,128)(2,1)} %pad_maximum_fusion.4), channel_id=1, source_target_pairs={{0,4},{2,6},{4,8},{6,10},{8,12},{10,14},{12,16},{14,18},{16,20},{1... | collective-permute-start | bytes 6291464 | tf_op jit(solution)/shard_map/ppermute | solution.py:19
  136.6 52.1 %collective-permute-done.5 = bf16[256,2048]{0,1:T(8,128)(2,1)} collective-permute-done((bf16[256,2048]{0,1:T(8,128)(2,1)S(1)}, bf16[256,2048]{0,1:T(8,128)(2,1)}, u32[]{:S(2)}, u32[]{:S(2)}) %collective-permute-start.5) | collective-permute-done | bytes 1048608 | tf_op jit(solution)/shard_map/ppermute | solution.py:19
  191.5 25.7 %collective-permute-start.6 = (bf16[512,2048]{0,1:T(8,128)(2,1)}, bf16[512,2048]{0,1:T(8,128)(2,1)S(1)}, u32[]{:S(2)}, u32[]{:S(2)}) collective-permute-start(bf16[512,2048]{0,1:T(8,128)(2,1)} %pad_maximum_fusion.5), channel_id=1, source_target_pairs={{0,4},{2,6},{4,8},{6,10},{8,12},{10,14},{12,16},{14,18},{16,20},{1... | collective-permute-start | bytes 6291464 | tf_op jit(solution)/shard_map/ppermute | solution.py:19
  229.1 28.6 %collective-permute-start.4 = (bf16[1024,2048]{0,1:T(8,128)(2,1)}, bf16[1024,2048]{0,1:T(8,128)(2,1)}, u32[]{:S(2)}, u32[]{:S(2)}) collective-permute-start(bf16[1024,2048]{0,1:T(8,128)(2,1)} %pad_maximum_fusion.2), channel_id=1, source_target_pairs={{0,8},{2,10},{4,12},{6,14},{8,16},{10,18},{12,20},{14,22},{16,24},... | collective-permute-start | bytes 12582920 | tf_op jit(solution)/shard_map/ppermute | solution.py:19
  265.3 36.8 %collective-permute-start.7 = (bf16[1024,2048]{0,1:T(8,128)(2,1)}, bf16[1024,2048]{0,1:T(8,128)(2,1)}, u32[]{:S(2)}, u32[]{:S(2)}) collective-permute-start(bf16[1024,2048]{0,1:T(8,128)(2,1)} %pad_maximum_fusion.3), channel_id=1, source_target_pairs={{0,8},{2,10},{4,12},{6,14},{8,16},{10,18},{12,20},{14,22},{16,24},... | collective-permute-start | bytes 12582920 | tf_op jit(solution)/shard_map/ppermute | solution.py:19
  304.5 8.4 pad_maximum_fusion
  312.8 8.5 pad_maximum_fusion.1
  321.3 477.5 %while.16 = (s32[]{:T(128)}, f32[16,1024,128]{2,0,1:T(8,128)}, f32[16,1024]{1,0:T(8,128)S(1)}, f32[16,1024]{1,0:T(8,128)S(1)}, s32[16]{0:T(128)S(1)}, /*index=5*...) while((s32[]{:T(128)}, f32[16,1024,128]{2,0,1:T(8,128)}, ...), condition=%wide.region_3.4_spmd.clone.clone, body=%wide.region_0.3_spmd.clone.sunk.clone | while | flops 1113585664 | bytes 61680860 | solution.py:95
  330.4 14.9 %dynamic_update_slice.20 = f32[16,1024,128]{2,0,1:T(8,128)} dynamic-update-slice(f32[16,1024,128]{2,0,1:T(8,128)} %get-tuple-element.285, f32[1,1024,128]{2,0,1:T(1,128)S(1)} %bitcast.97, s32[]{:T(128)} %get-tuple-element.284, s32[]{:T(128)} %constant.154.clone.1..sunk.1, s32[]{:T(128)} %constant.154.clone.1..sunk.1) | dynamic-update-slice | bytes 1048580 | tf_op jit(solution)/shard_map/while/body/jit(dynamic_update_index_in_dim)/dynamic_update_slice | solution.py:95
  345.3 5.6 fusion.103
  360.3 14.9 %dynamic_update_slice.20 = f32[16,1024,128]{2,0,1:T(8,128)} dynamic-update-slice(f32[16,1024,128]{2,0,1:T(8,128)} %get-tuple-element.285, f32[1,1024,128]{2,0,1:T(1,128)S(1)} %bitcast.97, s32[]{:T(128)} %get-tuple-element.284, s32[]{:T(128)} %constant.154.clone.1..sunk.1, s32[]{:T(128)} %constant.154.clone.1..sunk.1) | dynamic-update-slice | bytes 1048580 | tf_op jit(solution)/shard_map/while/body/jit(dynamic_update_index_in_dim)/dynamic_update_slice | solution.py:95
  375.2 5.6 fusion.103
  390.1 14.9 %dynamic_update_slice.20 = f32[16,1024,128]{2,0,1:T(8,128)} dynamic-update-slice(f32[16,1024,128]{2,0,1:T(8,128)} %get-tuple-element.285, f32[1,1024,128]{2,0,1:T(1,128)S(1)} %bitcast.97, s32[]{:T(128)} %get-tuple-element.284, s32[]{:T(128)} %constant.154.clone.1..sunk.1, s32[]{:T(128)} %constant.154.clone.1..sunk.1) | dynamic-update-slice | bytes 1048580 | tf_op jit(solution)/shard_map/while/body/jit(dynamic_update_index_in_dim)/dynamic_update_slice | solution.py:95
  405.0 5.6 fusion.103
  420.0 14.9 %dynamic_update_slice.20 = f32[16,1024,128]{2,0,1:T(8,128)} dynamic-update-slice(f32[16,1024,128]{2,0,1:T(8,128)} %get-tuple-element.285, f32[1,1024,128]{2,0,1:T(1,128)S(1)} %bitcast.97, s32[]{:T(128)} %get-tuple-element.284, s32[]{:T(128)} %constant.154.clone.1..sunk.1, s32[]{:T(128)} %constant.154.clone.1..sunk.1) | dynamic-update-slice | bytes 1048580 | tf_op jit(solution)/shard_map/while/body/jit(dynamic_update_index_in_dim)/dynamic_update_slice | solution.py:95
  434.8 5.6 fusion.103
  449.8 14.9 %dynamic_update_slice.20 = f32[16,1024,128]{2,0,1:T(8,128)} dynamic-update-slice(f32[16,1024,128]{2,0,1:T(8,128)} %get-tuple-element.285, f32[1,1024,128]{2,0,1:T(1,128)S(1)} %bitcast.97, s32[]{:T(128)} %get-tuple-element.284, s32[]{:T(128)} %constant.154.clone.1..sunk.1, s32[]{:T(128)} %constant.154.clone.1..sunk.1) | dynamic-update-slice | bytes 1048580 | tf_op jit(solution)/shard_map/while/body/jit(dynamic_update_index_in_dim)/dynamic_update_slice | solution.py:95
  464.7 5.6 fusion.103
  479.7 14.9 %dynamic_update_slice.20 = f32[16,1024,128]{2,0,1:T(8,128)} dynamic-update-slice(f32[16,1024,128]{2,0,1:T(8,128)} %get-tuple-element.285, f32[1,1024,128]{2,0,1:T(1,128)S(1)} %bitcast.97, s32[]{:T(128)} %get-tuple-element.284, s32[]{:T(128)} %constant.154.clone.1..sunk.1, s32[]{:T(128)} %constant.154.clone.1..sunk.1) | dynamic-update-slice | bytes 1048580 | tf_op jit(solution)/shard_map/while/body/jit(dynamic_update_index_in_dim)/dynamic_update_slice | solution.py:95
  494.5 5.6 fusion.103
  509.5 14.9 %dynamic_update_slice.20 = f32[16,1024,128]{2,0,1:T(8,128)} dynamic-update-slice(f32[16,1024,128]{2,0,1:T(8,128)} %get-tuple-element.285, f32[1,1024,128]{2,0,1:T(1,128)S(1)} %bitcast.97, s32[]{:T(128)} %get-tuple-element.284, s32[]{:T(128)} %constant.154.clone.1..sunk.1, s32[]{:T(128)} %constant.154.clone.1..sunk.1) | dynamic-update-slice | bytes 1048580 | tf_op jit(solution)/shard_map/while/body/jit(dynamic_update_index_in_dim)/dynamic_update_slice | solution.py:95
  524.4 5.6 fusion.103
  539.3 14.9 %dynamic_update_slice.20 = f32[16,1024,128]{2,0,1:T(8,128)} dynamic-update-slice(f32[16,1024,128]{2,0,1:T(8,128)} %get-tuple-element.285, f32[1,1024,128]{2,0,1:T(1,128)S(1)} %bitcast.97, s32[]{:T(128)} %get-tuple-element.284, s32[]{:T(128)} %constant.154.clone.1..sunk.1, s32[]{:T(128)} %constant.154.clone.1..sunk.1) | dynamic-update-slice | bytes 1048580 | tf_op jit(solution)/shard_map/while/body/jit(dynamic_update_index_in_dim)/dynamic_update_slice | solution.py:95
  554.2 5.6 fusion.103
  569.2 14.9 %dynamic_update_slice.20 = f32[16,1024,128]{2,0,1:T(8,128)} dynamic-update-slice(f32[16,1024,128]{2,0,1:T(8,128)} %get-tuple-element.285, f32[1,1024,128]{2,0,1:T(1,128)S(1)} %bitcast.97, s32[]{:T(128)} %get-tuple-element.284, s32[]{:T(128)} %constant.154.clone.1..sunk.1, s32[]{:T(128)} %constant.154.clone.1..sunk.1) | dynamic-update-slice | bytes 1048580 | tf_op jit(solution)/shard_map/while/body/jit(dynamic_update_index_in_dim)/dynamic_update_slice | solution.py:95
  584.1 5.6 fusion.103
  599.0 14.9 %dynamic_update_slice.20 = f32[16,1024,128]{2,0,1:T(8,128)} dynamic-update-slice(f32[16,1024,128]{2,0,1:T(8,128)} %get-tuple-element.285, f32[1,1024,128]{2,0,1:T(1,128)S(1)} %bitcast.97, s32[]{:T(128)} %get-tuple-element.284, s32[]{:T(128)} %constant.154.clone.1..sunk.1, s32[]{:T(128)} %constant.154.clone.1..sunk.1) | dynamic-update-slice | bytes 1048580 | tf_op jit(solution)/shard_map/while/body/jit(dynamic_update_index_in_dim)/dynamic_update_slice | solution.py:95
  628.9 14.9 %dynamic_update_slice.20 = f32[16,1024,128]{2,0,1:T(8,128)} dynamic-update-slice(f32[16,1024,128]{2,0,1:T(8,128)} %get-tuple-element.285, f32[1,1024,128]{2,0,1:T(1,128)S(1)} %bitcast.97, s32[]{:T(128)} %get-tuple-element.284, s32[]{:T(128)} %constant.154.clone.1..sunk.1, s32[]{:T(128)} %constant.154.clone.1..sunk.1) | dynamic-update-slice | bytes 1048580 | tf_op jit(solution)/shard_map/while/body/jit(dynamic_update_index_in_dim)/dynamic_update_slice | solution.py:95
  658.7 14.9 %dynamic_update_slice.20 = f32[16,1024,128]{2,0,1:T(8,128)} dynamic-update-slice(f32[16,1024,128]{2,0,1:T(8,128)} %get-tuple-element.285, f32[1,1024,128]{2,0,1:T(1,128)S(1)} %bitcast.97, s32[]{:T(128)} %get-tuple-element.284, s32[]{:T(128)} %constant.154.clone.1..sunk.1, s32[]{:T(128)} %constant.154.clone.1..sunk.1) | dynamic-update-slice | bytes 1048580 | tf_op jit(solution)/shard_map/while/body/jit(dynamic_update_index_in_dim)/dynamic_update_slice | solution.py:95
  688.6 14.9 %dynamic_update_slice.20 = f32[16,1024,128]{2,0,1:T(8,128)} dynamic-update-slice(f32[16,1024,128]{2,0,1:T(8,128)} %get-tuple-element.285, f32[1,1024,128]{2,0,1:T(1,128)S(1)} %bitcast.97, s32[]{:T(128)} %get-tuple-element.284, s32[]{:T(128)} %constant.154.clone.1..sunk.1, s32[]{:T(128)} %constant.154.clone.1..sunk.1) | dynamic-update-slice | bytes 1048580 | tf_op jit(solution)/shard_map/while/body/jit(dynamic_update_index_in_dim)/dynamic_update_slice | solution.py:95
  718.4 14.9 %dynamic_update_slice.20 = f32[16,1024,128]{2,0,1:T(8,128)} dynamic-update-slice(f32[16,1024,128]{2,0,1:T(8,128)} %get-tuple-element.285, f32[1,1024,128]{2,0,1:T(1,128)S(1)} %bitcast.97, s32[]{:T(128)} %get-tuple-element.284, s32[]{:T(128)} %constant.154.clone.1..sunk.1, s32[]{:T(128)} %constant.154.clone.1..sunk.1) | dynamic-update-slice | bytes 1048580 | tf_op jit(solution)/shard_map/while/body/jit(dynamic_update_index_in_dim)/dynamic_update_slice | solution.py:95
  748.3 14.9 %dynamic_update_slice.20 = f32[16,1024,128]{2,0,1:T(8,128)} dynamic-update-slice(f32[16,1024,128]{2,0,1:T(8,128)} %get-tuple-element.285, f32[1,1024,128]{2,0,1:T(1,128)S(1)} %bitcast.97, s32[]{:T(128)} %get-tuple-element.284, s32[]{:T(128)} %constant.154.clone.1..sunk.1, s32[]{:T(128)} %constant.154.clone.1..sunk.1) | dynamic-update-slice | bytes 1048580 | tf_op jit(solution)/shard_map/while/body/jit(dynamic_update_index_in_dim)/dynamic_update_slice | solution.py:95
  778.1 14.9 %dynamic_update_slice.20 = f32[16,1024,128]{2,0,1:T(8,128)} dynamic-update-slice(f32[16,1024,128]{2,0,1:T(8,128)} %get-tuple-element.285, f32[1,1024,128]{2,0,1:T(1,128)S(1)} %bitcast.97, s32[]{:T(128)} %get-tuple-element.284, s32[]{:T(128)} %constant.154.clone.1..sunk.1, s32[]{:T(128)} %constant.154.clone.1..sunk.1) | dynamic-update-slice | bytes 1048580 | tf_op jit(solution)/shard_map/while/body/jit(dynamic_update_index_in_dim)/dynamic_update_slice | solution.py:95
  798.9 6.5 copy.95
  805.4 6.4 copy.109
  811.8 24.6 %fusion.12 = (f32[16,256]{1,0:T(8,128)S(1)}, f32[16,256,2048]{2,1,0:T(8,128)}) fusion(s32[16,256]{1,0:T(8,128)S(1)} %broadcast_add_fusion.2, s32[16,2048]{1,0:T(8,128)S(1)} %broadcast_add_fusion, pred[16,2048]{1,0:T(8,128)(4,1)S(1)} %broadcast_compare_fusion, bf16[256,16,128]{2,0,1:T(8,128)(2,1)} %copy.98, bf16[256,16,128]{2,0,1:T(8,128)(2,1)} %copy.97, ...), kind=kOutput, calls=%fused_computation.17 | convolution fusion | flops 2222977024 | bytes 43188224 | tf_op jit(solution)/shard_map/qhd,khd->hqk/dot_general | solution.py:23
  836.5 17.3 %fusion.13 = f32[16,256,128]{2,1,0:T(8,128)S(1)} fusion(f32[16,256,2048]{2,1,0:T(8,128)} %get-tuple-element.167, f32[16,256]{1,0:T(8,128)S(1)} %get-tuple-element.166, s32[16,256]{1,0:T(8,128)S(1)} %broadcast_add_fusion.2, s32[16,2048]{1,0:T(8,128)S(1)} %broadcast_add_fusion, pred[16,2048]{1,0:T(8,128)(4,1)S(1)} %broadcast_compare_fusion, ...), kind=kOutput, calls=%fused_computation.18 | convolution fusion | flops 2239758336 | bytes 44236800 | tf_op jit(solution)/shard_map/hqk,khd->hqd/dot_general | solution.py:28
  855.0 17.5 %fusion.15 = f32[16,256]{1,0:T(8,128)S(1)} fusion(f32[16,256]{1,0:T(8,128)S(1)} %get-tuple-element.166, f32[16,256,2048]{2,1,0:T(8,128)} %get-tuple-element.167, pred[16,2048]{1,0:T(8,128)(4,1)S(1)} %broadcast_compare_fusion, s32[16,256]{1,0:T(8,128)S(1)} %broadcast_add_fusion.2, s32[16,2048]{1,0:T(8,128)S(1)} %broadcast_add_fusion), kind=kLoop, calls=%fused_computation.20 | loop fusion | flops 58716160 | bytes 33767424 | tf_op jit(solution)/shard_map/reduce_sum | solution.py:27
  873.2 6.4 copy.103
  889.5 6.6 copy.116
  896.2 6.0 fusion.43
  902.9 15.5 %fusion.36 = bf16[16,1024,128]{2,0,1:T(8,128)(2,1)} fusion(f32[16,1024,128]{2,1,0:T(8,128)S(1)} %bitcast.92, f32[16,1024,128]{2,0,1:T(8,128)S(1)} %bitcast.102, f32[16,1024]{0,1:T(8,128)S(1)} %copy-done.8, f32[16,1024]{0,1:T(8,128)S(1)} %copy-done.7, f32[16,1024]{0,1:T(8,128)S(1)} %copy.114, f32[16,256,128]{2,0,1:T(8,128)S(1)} %copy.113, ...), kind=kLoop, calls=%fused_computation.45 | loop fusion | flops 18874368 | bytes 23363584 | tf_op jit(solution)/shard_map/convert_element_type | solution.py:167
  918.4 6.7 copy.124
  925.1 23.3 %convolution_convert_fusion = bf16[1024,4096]{1,0:T(8,128)(2,1)} fusion(bf16[1024,2048]{0,1:T(8,128)(2,1)} %bitcast.106, bf16[2048,4096]{1,0:T(8,128)(2,1)} %param.9), kind=kOutput, calls=%fused_computation.46 | convolution fusion | flops 17184063488 | bytes 29360128 | tf_op jit(solution)/shard_map/dot_general | solution.py:169
  948.4 96.2 %reduce-scatter.2.cloned.1.call-done = bf16[1024,2048]{1,0:T(8,128)(2,1)} async-done(((bf16[1024,4096]{1,0:T(8,128)(2,1)}), bf16[1024,2048]{1,0:T(8,128)(2,1)}) %reduce-scatter.2.cloned.1.call-update) | async-done | bytes 4194320 | tf_op jit(solution)/shard_map/reduce_scatter | solution.py:170
  (244 shorter events, 245.1 us)
Async XLA Ops:
  6.5 866.7 %all-gather.3.cloned.1.call-start = ((), (), s32[]{:S(2)}) async-start(), calls=%async_computation.1 | async-start | bytes 4456448 | tf_op jit(solution)/shard_map/all_gather | solution.py:135
  6.5 3.8 copy-start.5
  6.6 5.2 copy-start.6
  10.3 3.0 copy-start.1
  11.7 8.0 copy-start.2
  13.2 6.6 copy-start.3
  20.6 869.0 %all-gather.5.cloned.1.call-start = ((), (), s32[]{:S(2)}) async-start(), calls=%async_computation.2 | async-start | bytes 4456448 | tf_op jit(solution)/shard_map/all_gather | solution.py:136
  20.6 283.8 %collective-permute-start = (bf16[1024,2048]{1,0:T(8,128)(2,1)}, bf16[1024,2048]{1,0:T(8,128)(2,1)}, u32[]{:S(2)}, u32[]{:S(2)}) collective-permute-start(bf16[1024,2048]{1,0:T(8,128)(2,1)} %param.7), channel_id=1, source_target_pairs={{0,2},{2,4},{4,6},{6,8},{8,10},{10,12},{12,14},{14,16},{16,18},{18... | collective-permute-start | bytes 12582920 | tf_op jit(solution)/shard_map/ppermute | solution.py:19
  37.5 61.5 %collective-permute-start.2 = (bf16[256,2048]{0,1:T(8,128)(2,1)}, bf16[256,2048]{0,1:T(8,128)(2,1)}, u32[]{:S(2)}, u32[]{:S(2)}) collective-permute-start(bf16[256,2048]{0,1:T(8,128)(2,1)} %bitcast.1), channel_id=1, source_target_pairs={{0,2},{2,4},{4,6},{6,8},{8,10},{10,12},{12,14},{14,16},{16,18},{18... | collective-permute-start | bytes 3145736 | tf_op jit(solution)/shard_map/ppermute | solution.py:19
  39.4 273.4 %collective-permute-start.1 = (bf16[1024,2048]{1,0:T(8,128)(2,1)}, bf16[1024,2048]{1,0:T(8,128)(2,1)}, u32[]{:S(2)}, u32[]{:S(2)}) collective-permute-start(bf16[1024,2048]{1,0:T(8,128)(2,1)} %param.8), channel_id=1, source_target_pairs={{0,2},{2,4},{4,6},{6,8},{8,10},{10,12},{12,14},{14,16},{16,18},{18... | collective-permute-start | bytes 12582920 | tf_op jit(solution)/shard_map/ppermute | solution.py:19
  43.8 145.0 %collective-permute-start.5 = (bf16[256,2048]{0,1:T(8,128)(2,1)S(1)}, bf16[256,2048]{0,1:T(8,128)(2,1)}, u32[]{:S(2)}, u32[]{:S(2)}) collective-permute-start(bf16[256,2048]{0,1:T(8,128)(2,1)S(1)} %bitcast.98), channel_id=1, source_target_pairs={{0,2},{2,4},{4,6},{6,8},{8,10},{10,12},{12,14},{14,16},{16,18},{18... | collective-permute-start | bytes 3145736 | tf_op jit(solution)/shard_map/ppermute | solution.py:19
  46.5 998.1 %reduce-scatter.2.cloned.1.call-start = ((), (), s32[]{:S(2)}) async-start(), calls=%async_computation.3 | async-start | bytes 12582912 | tf_op jit(solution)/shard_map/reduce_scatter | solution.py:170
  102.0 123.3 %collective-permute-start.3 = (bf16[512,2048]{0,1:T(8,128)(2,1)}, bf16[512,2048]{0,1:T(8,128)(2,1)}, u32[]{:S(2)}, u32[]{:S(2)}) collective-permute-start(bf16[512,2048]{0,1:T(8,128)(2,1)} %pad_maximum_fusion.4), channel_id=1, source_target_pairs={{0,4},{2,6},{4,8},{6,10},{8,12},{10,14},{12,16},{14,18},{16,20},{1... | collective-permute-start | bytes 6291464 | tf_op jit(solution)/shard_map/ppermute | solution.py:19
  134.6 54.2 %copy-start.10 = (pred[16,256,4]{0,2,1:T(4,128)(4,1)}, pred[16,256,4]{0,2,1:T(4,128)(4,1)S(1)}, u32[]{:S(2)}) copy-start(pred[16,256,4]{0,2,1:T(4,128)(4,1)S(1)} %broadcast_in_dim.202) | copy-start | bytes 49156
  135.8 82.9 %copy-start.16 = (pred[16,1024]{1,0:T(8,128)(4,1)}, pred[16,1024]{1,0:T(8,128)(4,1)S(1)}, u32[]{:S(2)}) copy-start(pred[16,1024]{1,0:T(8,128)(4,1)S(1)} %broadcast_in_dim.209) | copy-start | bytes 49156
  191.5 70.2 %collective-permute-start.6 = (bf16[512,2048]{0,1:T(8,128)(2,1)}, bf16[512,2048]{0,1:T(8,128)(2,1)S(1)}, u32[]{:S(2)}, u32[]{:S(2)}) collective-permute-start(bf16[512,2048]{0,1:T(8,128)(2,1)} %pad_maximum_fusion.5), channel_id=1, source_target_pairs={{0,4},{2,6},{4,8},{6,10},{8,12},{10,14},{12,16},{14,18},{16,20},{1... | collective-permute-start | bytes 6291464 | tf_op jit(solution)/shard_map/ppermute | solution.py:19
  229.1 569.7 %collective-permute-start.4 = (bf16[1024,2048]{0,1:T(8,128)(2,1)}, bf16[1024,2048]{0,1:T(8,128)(2,1)}, u32[]{:S(2)}, u32[]{:S(2)}) collective-permute-start(bf16[1024,2048]{0,1:T(8,128)(2,1)} %pad_maximum_fusion.2), channel_id=1, source_target_pairs={{0,8},{2,10},{4,12},{6,14},{8,16},{10,18},{12,20},{14,22},{16,24},... | collective-permute-start | bytes 12582920 | tf_op jit(solution)/shard_map/ppermute | solution.py:19
  265.3 540.1 %collective-permute-start.7 = (bf16[1024,2048]{0,1:T(8,128)(2,1)}, bf16[1024,2048]{0,1:T(8,128)(2,1)}, u32[]{:S(2)}, u32[]{:S(2)}) collective-permute-start(bf16[1024,2048]{0,1:T(8,128)(2,1)} %pad_maximum_fusion.3), channel_id=1, source_target_pairs={{0,8},{2,10},{4,12},{6,14},{8,16},{10,18},{12,20},{14,22},{16,24},... | collective-permute-start | bytes 12582920 | tf_op jit(solution)/shard_map/ppermute | solution.py:19
  326.1 4.3 copy-start
  356.0 4.3 copy-start
  385.8 4.3 copy-start
  415.7 4.3 copy-start
  445.5 4.3 copy-start
  475.3 4.3 copy-start
  505.2 4.3 copy-start
  535.0 4.3 copy-start
  564.9 4.3 copy-start
  594.7 4.3 copy-start
  624.6 4.3 copy-start
  654.4 4.3 copy-start
  684.3 4.3 copy-start
  714.1 4.3 copy-start
  743.9 4.3 copy-start
  773.8 4.3 copy-start
  798.8 13.0 %copy-start.9 = (bf16[512,16,128]{2,0,1:T(8,128)(2,1)S(1)}, bf16[512,16,128]{2,0,1:T(8,128)(2,1)}, u32[]{:S(2)}) copy-start(bf16[512,16,128]{2,0,1:T(8,128)(2,1)} %copy.96) | copy-start | bytes 6291460
  798.8 12.9 %copy-start.12 = (bf16[256,16,128]{2,1,0:T(8,128)(2,1)S(1)}, bf16[256,16,128]{2,1,0:T(8,128)(2,1)}, u32[]{:S(2)}) copy-start(bf16[256,16,128]{2,1,0:T(8,128)(2,1)} %get-tuple-element.133) | copy-start | bytes 3145732
  872.5 7.1 copy-start.13
  872.5 7.1 copy-start.14
  872.6 7.1 copy-start.18
  879.6 7.4 copy-start.17
  879.6 7.4 copy-start.19
  882.7 2.0 copy-start.4
  896.1 6.7 slice-start
  896.1 6.7 slice-start.1
  896.1 6.7 copy-start.7
  896.2 6.7 copy-start.8
  896.2 6.7 copy-start.11
  896.2 6.7 copy-start.15
Sparse Core Ops, SparseCore 0:
  20.7 59.7 all-gather.2
  82.7 61.7 all-gather.4
  948.5 96.0 reduce-scatter.1
where the time goes:
time: 1060 us; the launch traced here: 1050 us
  local copies, waits for them, and re-layouts  318 us (30%)
  waiting for transfers between devices  203 us (19%)
  matrix products  199 us (19%)
  other arithmetic  173 us (16%)
  starting transfers between devices  133 us (13%)
  between operations  13.9 us (1%)
  loops' own time  11.3 us (1%)
    dynamic_update_slice x48, local copies, waits for them, and re-layouts, shards(): near_state = lax.map(near_head, jnp.arange(heads_here))  242 us
    ppermute x8, starting transfers between devices, passed_along(): lax.ppermute(value, axis, [(source, source + steps) for source in range(l...  133 us
    reduce_sum x17, other arithmetic, attend_block(): total = jnp.sum(weights, axis=-1)  107 us
    ppermute x8, waiting for transfers between devices, passed_along(): lax.ppermute(value, axis, [(source, source + steps) for source in range(l...  106 us
    reduce_scatter x1, waiting for transfers between devices, shards(): lax.psum_scatter(terms.astype(jnp.bfloat16), 'head', scatter_dimension=1,...  96.2 us
    dot_general x17, matrix products, attend_block(): jnp.einsum('hqk,khd->hqd', weights.astype(jnp.bfloat16), value_rows, pref...  85.8 us
    dot_general x17, matrix products, attend_block(): jnp.einsum('qhd,khd->hqk', query, key_rows, preferred_element_type=jnp.fl...  81.3 us
    dot_general x1, matrix products, shards(): terms = jnp.dot(attended, out_weight, preferred_element_type=jnp.float32)  23.3 us
  transfers between devices with their start and end apart: 11, of which 4 were waited for; matrix products, arithmetic and copies ran while one was open for 59% of the time, Pallas kernels for 0%

commit v1 on v0

--- a/solution.py
+++ b/solution.py
@@ -1,8 +1,11 @@
+import functools
 import math
 
 import jax
 import jax.numpy as jnp
 from jax import lax
+from jax.experimental import pallas as pl
+from jax.experimental.pallas import tpu as pltpu
 from jax.sharding import PartitionSpec as P
 
 HEAD_DIM = 128
@@ -11,6 +14,453 @@
 
 
 NEG_FILL = -1e30
+LOG2_SCALE = math.log2(math.e) / math.sqrt(HEAD_DIM)
+CHUNK = 256
+GROUP = 8
+MID_ROWS = CHUNK // 4
+FAR_ROWS = CHUNK // 16
+STAT_ROWS = 16
+VMEM_BYTES = 50 * 2**20
+F32 = jnp.float32
+BF16 = jnp.bfloat16
+
+
+def iota(shape, dim):
+    return lax.broadcasted_iota(jnp.int32, shape, dim)
+
+
+def token_of_row(row):
+    return 16 * (row & 15) + 4 * ((row >> 4) & 3) + (row >> 6)
+
+
+def mid_of_row(row):
+    return (row >> 6) * 64 + 4 * (row & 15) + ((row >> 4) & 3)
+
+
+def dot(lhs, rhs):
+    return lax.dot_general(lhs, rhs, (((1,), (0,)), ((), ())), preferred_element_type=F32)
+
+
+def dot_t(lhs, rhs):
+    return lax.dot_general(lhs, rhs, (((1,), (1,)), ((), ())), preferred_element_type=F32)
+
+
+def with_ones(values):
+    return jnp.concatenate([values, jnp.ones_like(values)], axis=1)
+
+
+def attend(query, parts):
+    scores = []
+    peak = None
+    for keys, _, mask in parts:
+        score = dot_t(query, keys)
+        if mask is not None:
+            score = jnp.where(mask, score, NEG_FILL)
+        scores.append(score)
+        top = jnp.max(score, axis=1, keepdims=True)
+        peak = top if peak is None else jnp.maximum(peak, top)
+    acc = None
+    for score, (_, values, _) in zip(scores, parts):
+        weights = jnp.exp2((score - peak) * LOG2_SCALE).astype(BF16)
+        term = dot(weights, values)
+        acc = term if acc is None else acc + term
+    total = acc[:, HEAD_DIM:]
+    return acc[:, :HEAD_DIM] / total, peak * LOG2_SCALE + jnp.log2(total)
+
+
+def merge(out_a, lse_a, out_b, lse_b):
+    top = jnp.maximum(lse_a, lse_b)
+    fac_a = jnp.exp2(lse_a - top)
+    fac_b = jnp.exp2(lse_b - top)
+    total = fac_a + fac_b
+    return (out_a * fac_a + out_b * fac_b) / total, top + jnp.log2(total)
+
+
+def prep_kv_kernel(place, k_ref, v_ref, *outs):
+    me = place[0]
+    for d in range(GROUP):
+        owner = me ^ d
+        for e in range(2):
+            residue = 2 * (owner & 1) + e
+            row = iota((MID_ROWS, CHUNK), 0)
+            token = 16 * (row & 15) + 4 * (row >> 4) + residue
+            pick = (token == iota((MID_ROWS, CHUNK), 1)).astype(F32).astype(BF16)
+            column = pl.multiple_of(owner * 256 + e * 128, 128)
+            for a, source in enumerate((k_ref, v_ref)):
+                outs[d][a, :, e * 128 : (e + 1) * 128] = dot(pick, source[:, pl.ds(column, 128)]).astype(BF16)
+        start = pl.multiple_of(((owner >> 1) & 3) * FAR_ROWS, FAR_ROWS)
+        for a in range(2):
+            outs[GROUP + d][a] = outs[d][a, pl.ds(start, FAR_ROWS), :]
+
+
+def prep_q_kernel(place, q_ref, rows_ref, *outs):
+    me = place[0]
+    row = iota((CHUNK, CHUNK), 0)
+    pick = (token_of_row(row) == iota((CHUNK, CHUNK), 1)).astype(F32).astype(BF16)
+    rows_ref[...] = dot(pick, q_ref[...]).astype(BF16)
+    for d in range(GROUP):
+        owner = me ^ d
+        for e in range(2):
+            start = pl.multiple_of((2 * (owner & 1) + e) * MID_ROWS, MID_ROWS)
+            column = pl.multiple_of(owner * 256 + e * 128, 128)
+            outs[d][:, e * 128 : (e + 1) * 128] = rows_ref[pl.ds(start, MID_ROWS), pl.ds(column, 128)]
+
+
+def put_lane(ref, rows, lane, value):
+    ref[rows, :] = jnp.where(iota((CHUNK, 128), 1) == lane, value, ref[rows, :])
+
+
+def get_lane(block, lane):
+    return jnp.sum(jnp.where(iota(block.shape, 1) == lane, block, 0.0), axis=1, keepdims=True)
+
+
+def near_own_kernel(chunks, q_ref, k_ref, v_ref, o_ref, lse_ref):
+    head = pl.program_id(0)
+
+    @pl.when(head == 0)
+    def _():
+        lse_ref[...] = jnp.zeros_like(lse_ref)
+
+    mask = token_of_row(iota((CHUNK, CHUNK), 0)) >= iota((CHUNK, CHUNK), 1)
+    values = with_ones(v_ref[...])
+    for c in range(chunks):
+        here = slice(c * CHUNK, (c + 1) * CHUNK)
+        parts = [(k_ref[here, :], values[here], mask)]
+        if c:
+            parts.append((k_ref[: c * CHUNK, :], values[: c * CHUNK], None))
+        out, lse = attend(q_ref[here, :], parts)
+        o_ref[here, :] = out.astype(BF16)
+        put_lane(lse_ref, here, head, lse)
+
+
+def near_prev_kernel(chunks, place, q_ref, k_ref, v_ref, own_o, own_lse, o_ref, lse_ref):
+    head = pl.program_id(0)
+    second = (place[0] & 1) == 1
+
+    @pl.when(head == 0)
+    def _():
+        lse_ref[...] = own_lse[...]
+
+    @pl.when(jnp.logical_not(second))
+    def _():
+        o_ref[...] = own_o[...]
+
+    @pl.when(second)
+    def _():
+        values = with_ones(v_ref[...])
+        keys = k_ref[...]
+        for c in range(chunks):
+            here = slice(c * CHUNK, (c + 1) * CHUNK)
+            out, lse = attend(q_ref[here, :], [(keys, values, None)])
+            out, lse = merge(
+                out, lse, own_o[here, :].astype(F32), get_lane(own_lse[here, :], head)
+            )
+            o_ref[here, :] = out.astype(BF16)
+            put_lane(lse_ref, here, head, lse)
+
+
+def mid_kernel(rows, place, *refs):
+    kv_in, q_in, far_in = refs[:GROUP], refs[GROUP : 2 * GROUP], refs[2 * GROUP : 3 * GROUP]
+    outs = refs[3 * GROUP : 4 * GROUP]
+    kv, q, far_kv, res, lses, sems = refs[4 * GROUP :]
+    me = place[0]
+    later = place[1]
+    copies = []
+    for d in range(GROUP):
+        owner = me ^ d
+        copies.append(pltpu.make_async_copy(kv_in[d], kv.at[owner], sems.at[d]))
+        copies.append(pltpu.make_async_copy(q_in[d], q.at[owner], sems.at[GROUP + d]))
+        copies.append(pltpu.make_async_copy(far_in[d], far_kv.at[owner], sems.at[2 * GROUP + d]))
+    for copy in copies:
+        copy.start()
+    for copy in copies:
+        copy.wait()
+    mask = mid_of_row(iota((rows, rows), 0)) >= mid_of_row(iota((rows, rows), 1))
+    for e in range(2):
+        lanes = slice(e * 128, (e + 1) * 128)
+        for i in range(GROUP):
+            parts = [(kv[i, 0, :, lanes], with_ones(kv[i, 1, :, lanes]), mask)]
+            if i:
+                parts.append(
+                    (
+                        kv[:i, 0, :, lanes].reshape(i * rows, 128),
+                        with_ones(kv[:i, 1, :, lanes].reshape(i * rows, 128)),
+                        None,
+                    )
+                )
+            out, lse = attend(q[i, :, lanes], parts)
+            res[e, i] = out
+            lses[e, i] = lse
+    start = pl.multiple_of(((me >> 1) & 3) * FAR_ROWS, FAR_ROWS)
+    chunks = rows // MID_ROWS
+    count = GROUP * chunks * FAR_ROWS
+    mask = iota((count, count), 0) >= iota((count, count), 1)
+    for e in range(2):
+        lanes = slice(e * 128, (e + 1) * 128)
+
+        def dilated(pick):
+            pieces = []
+            for i in range(GROUP):
+                for c in range(chunks):
+                    pieces.append(pick(i, pl.ds(start + c * MID_ROWS, FAR_ROWS)))
+            return jnp.concatenate(pieces, axis=0)
+
+        query = dilated(lambda i, at: q[i, at, lanes])
+        keys = dilated(lambda i, at: kv[i, 0, at, lanes])
+        values = dilated(lambda i, at: kv[i, 1, at, lanes])
+        other_keys = far_kv[:, 0, :, lanes].reshape(count, 128)
+        other_values = far_kv[:, 1, :, lanes].reshape(count, 128)
+        out, lse = attend(
+            query,
+            [
+                (keys, with_ones(values), mask),
+                (other_keys, with_ones(other_values), jnp.broadcast_to(later == 1, (count, count))),
+            ],
+        )
+        for i in range(GROUP):
+            for c in range(chunks):
+                at = pl.ds(start + c * MID_ROWS, FAR_ROWS)
+                piece = slice((i * chunks + c) * FAR_ROWS, (i * chunks + c + 1) * FAR_ROWS)
+                res[e, i, at, :], lses[e, i, at, :] = merge(
+                    res[e, i, at, :], lses[e, i, at, :], out[piece], lse[piece]
+                )
+    lane = iota((rows, 128), 1)
+    stats = jnp.zeros((rows, 128), F32)
+    for d in range(GROUP):
+        for e in range(2):
+            stats = jnp.where(lane == 8 * d + e, lses[e, me ^ d], stats)
+    stats = jnp.transpose(stats)
+    high = stats.astype(BF16).astype(F32)
+    low = stats - high
+    for d in range(GROUP):
+        for e in range(2):
+            outs[d][:rows, e * 128 : (e + 1) * 128] = res[e, me ^ d].astype(BF16)
+        outs[d][rows:, :] = jnp.concatenate(
+            [high[8 * d : 8 * d + 8], low[8 * d : 8 * d + 8]], axis=0
+        ).astype(BF16)
+
+
+def combine_kernel(rows, chunk, place, o_ref, lse_ref, *refs):
+    back = refs[:GROUP]
+    w_ref, send_ref, att_ref, work = refs[GROUP:]
+
+    @pl.when(pl.program_id(0) == 0)
+    def _():
+        me = place[0]
+        work[...] = o_ref[...]
+        stats = []
+        for d in range(GROUP):
+            tile = back[d][rows:, :].astype(F32)
+            stats.append(tile[:8] + tile[8:])
+        stats.append(jnp.zeros((128 - 8 * GROUP, rows), F32))
+        stats = jnp.transpose(jnp.concatenate(stats, axis=0))
+        stats = stats[chunk * MID_ROWS : (chunk + 1) * MID_ROWS]
+        for d in range(GROUP):
+            owner = me ^ d
+            for e in range(2):
+                start = pl.multiple_of((2 * (owner & 1) + e) * MID_ROWS, MID_ROWS)
+                column = pl.multiple_of(owner * 256 + e * 128, 128)
+                at = (pl.ds(start, MID_ROWS), pl.ds(column, 128))
+                near = o_ref[at].astype(F32)
+                near_lse = get_lane(lse_ref[pl.ds(start, MID_ROWS), :], 2 * owner + e)
+                mid = back[d][chunk * MID_ROWS : (chunk + 1) * MID_ROWS, e * 128 : (e + 1) * 128]
+                mid_lse = stats[:, 8 * d + e : 8 * d + e + 1]
+                out, _ = merge(near, near_lse, mid.astype(F32), mid_lse)
+                work[at] = out.astype(BF16)
+        row = token_of_row(iota((CHUNK, CHUNK), 1))
+        pick = (row == iota((CHUNK, CHUNK), 0)).astype(F32).astype(BF16)
+        att_ref[...] = dot(pick, work[...]).astype(BF16)
+
+    send_ref[...] = dot(att_ref[...], w_ref[...]).astype(BF16)
+
+
+def project_kernel(place, att_ref, w_ref, out_ref):
+    out_ref[...] = dot(att_ref[...], w_ref[...]).astype(BF16)
+
+
+def params():
+    return pltpu.CompilerParams(vmem_limit_bytes=VMEM_BYTES)
+
+
+def fast_shards(queries, keys, values, out_weight):
+    tokens, width = queries.shape
+    heads = width // HEAD_DIM
+    features = out_weight.shape[1]
+    chunks = tokens // CHUNK
+    mid_rows = tokens // 4
+    far_rows = tokens // 16
+    seq_index = lax.axis_index("seq")
+    head_index = lax.axis_index("head")
+    place = jnp.stack([seq_index % GROUP, seq_index // GROUP, head_index]).astype(jnp.int32)
+    shape = jax.ShapeDtypeStruct
+
+    def spec(block, index):
+        return pl.BlockSpec(block, index)
+
+    seq_size = lax.axis_size("seq")
+    swaps = [[(i, i ^ d) for i in range(seq_size)] for d in range(GROUP)]
+    ahead = [[(i, (i ^ d) + GROUP) for i in range(seq_size - GROUP)] for d in range(GROUP)]
+
+    prev_k = lax.ppermute(keys, "seq", [(i, i + 1) for i in range(0, seq_size, 2)])
+    prev_v = lax.ppermute(values, "seq", [(i, i + 1) for i in range(0, seq_size, 2)])
+
+    blocks = pl.pallas_call(
+        prep_kv_kernel,
+        grid_spec=pltpu.PrefetchScalarGridSpec(
+            num_scalar_prefetch=1,
+            grid=(chunks,),
+            in_specs=[spec((CHUNK, width), lambda c, p: (c, 0))] * 2,
+            out_specs=[spec((2, MID_ROWS, 256), lambda c, p: (0, c, 0))] * GROUP
+            + [spec((2, FAR_ROWS, 256), lambda c, p: (0, c, 0))] * GROUP,
+        ),
+        out_shape=[shape((2, mid_rows, 256), BF16)] * GROUP + [shape((2, far_rows, 256), BF16)] * GROUP,
+        compiler_params=params(),
+        name="prep_kv",
+    )(place, keys, values)
+    kv_blocks, far_blocks = blocks[:GROUP], blocks[GROUP:]
+    kv_in = [kv_blocks[0]] + [lax.ppermute(kv_blocks[d], "seq", swaps[d]) for d in range(1, GROUP)]
+    far_in = [lax.ppermute(far_blocks[d], "seq", ahead[d]) for d in range(GROUP)]
+
+    ordered, *q_blocks = pl.pallas_call(
+        prep_q_kernel,
+        grid_spec=pltpu.PrefetchScalarGridSpec(
+            num_scalar_prefetch=1,
+            grid=(chunks,),
+            in_specs=[spec((CHUNK, width), lambda c, p: (c, 0))],
+            out_specs=[spec((CHUNK, width), lambda c, p: (c, 0))]
+            + [spec((MID_ROWS, 256), lambda c, p: (c, 0))] * GROUP,
+        ),
+        out_shape=[shape((tokens, width), BF16)] + [shape((mid_rows, 256), BF16)] * GROUP,
+        compiler_params=params(),
+        name="prep_q",
+    )(place, queries)
+    q_in = [q_blocks[0]] + [lax.ppermute(q_blocks[d], "seq", swaps[d]) for d in range(1, GROUP)]
+
+    column = spec((tokens, HEAD_DIM), lambda h, *_: (0, h))
+    whole_lse = spec((tokens, 128), lambda h, *_: (0, 0))
+    near_o, near_lse = pl.pallas_call(
+        functools.partial(near_own_kernel, chunks),
+        grid=(heads,),
+        in_specs=[column] * 3,
+        out_specs=[column, whole_lse],
+        out_shape=[shape((tokens, width), BF16), shape((tokens, 128), F32)],
+        compiler_params=params(),
+        cost_estimate=pl.CostEstimate(
+            flops=heads * 4 * tokens * tokens // 2 * HEAD_DIM, bytes_accessed=4 * tokens * width * 2, transcendentals=0
+        ),
+        name="near_own",
+    )(ordered, keys, values)
+    near_o, near_lse = pl.pallas_call(
+        functools.partial(near_prev_kernel, chunks),
+        grid_spec=pltpu.PrefetchScalarGridSpec(
+            num_scalar_prefetch=1,
+            grid=(heads,),
+            in_specs=[column] * 4 + [whole_lse],
+            out_specs=[column, whole_lse],
+        ),
+        out_shape=[shape((tokens, width), BF16), shape((tokens, 128), F32)],
+        compiler_params=params(),
+        cost_estimate=pl.CostEstimate(
+            flops=heads * 4 * tokens * tokens * HEAD_DIM, bytes_accessed=4 * tokens * width * 2, transcendentals=0
+        ),
+        name="near_prev",
+    )(place, ordered, prev_k, prev_v, near_o, near_lse)
+
+    anywhere = pl.BlockSpec(memory_space=pl.ANY)
+    back_rows = mid_rows + STAT_ROWS
+    back = pl.pallas_call(
+        functools.partial(mid_kernel, mid_rows),
+        grid_spec=pltpu.PrefetchScalarGridSpec(
+            num_scalar_prefetch=1,
+            grid=(1,),
+            in_specs=[anywhere] * (3 * GROUP),
+            out_specs=[spec((back_rows, 256), lambda s, p: (0, 0))] * GROUP,
+            scratch_shapes=[
+                pltpu.VMEM((GROUP, 2, mid_rows, 256), BF16),
+                pltpu.VMEM((GROUP, mid_rows, 256), BF16),
+                pltpu.VMEM((GROUP, 2, far_rows, 256), BF16),
+                pltpu.VMEM((2, GROUP, mid_rows, 128), F32),
+                pltpu.VMEM((2, GROUP, mid_rows, 128), F32),
+                pltpu.SemaphoreType.DMA((3 * GROUP,)),
+            ],
+        ),
+        out_shape=[shape((back_rows, 256), BF16)] * GROUP,
+        compiler_params=params(),
+        cost_estimate=pl.CostEstimate(
+            flops=2 * 4 * (GROUP * mid_rows) ** 2 // 2 * HEAD_DIM, bytes_accessed=4 * 2**20, transcendentals=0
+        ),
+        name="mid",
+    )(place, *kv_in, *q_in, *far_in)
+    returned = [back[0]] + [lax.ppermute(back[d], "seq", swaps[d]) for d in range(1, GROUP)]
+
+    half = features // 2
+    tile = 512
+    tiles = half // tile
+    received = []
+    attended = []
+    for c in range(chunks):
+        send, att = pl.pallas_call(
+            functools.partial(combine_kernel, mid_rows, c),
+            grid_spec=pltpu.PrefetchScalarGridSpec(
+                num_scalar_prefetch=1,
+                grid=(tiles,),
+                in_specs=[
+                    spec((CHUNK, width), lambda n, p, c=c: (c, 0)),
+                    spec((CHUNK, 128), lambda n, p, c=c: (c, 0)),
+                ]
+                + [spec((back_rows, 256), lambda n, p: (0, 0))] * GROUP
+                + [spec((width, tile), lambda n, p: (0, (1 - p[2]) * tiles + n))],
+                out_specs=[
+                    spec((CHUNK, tile), lambda n, p: (0, n)),
+                    spec((CHUNK, width), lambda n, p: (0, 0)),
+                ],
+                scratch_shapes=[pltpu.VMEM((CHUNK, width), BF16)],
+            ),
+            out_shape=[shape((CHUNK, half), BF16), shape((CHUNK, width), BF16)],
+            compiler_params=params(),
+            cost_estimate=pl.CostEstimate(
+                flops=2 * CHUNK * width * half, bytes_accessed=width * half * 2, transcendentals=0
+            ),
+            name="combine",
+        )(place, near_o, near_lse, *returned, out_weight)
+        received.append(lax.ppermute(send, "head", [(0, 1), (1, 0)]))
+        attended.append(att)
+    mixed = []
+    for c in range(chunks):
+        own = pl.pallas_call(
+            project_kernel,
+            grid_spec=pltpu.PrefetchScalarGridSpec(
+                num_scalar_prefetch=1,
+                grid=(tiles,),
+                in_specs=[
+                    spec((CHUNK, width), lambda n, p: (0, 0)),
+                    spec((width, tile), lambda n, p: (0, p[2] * tiles + n)),
+                ],
+                out_specs=spec((CHUNK, tile), lambda n, p: (0, n)),
+            ),
+            out_shape=shape((CHUNK, half), BF16),
+            compiler_params=params(),
+            cost_estimate=pl.CostEstimate(
+                flops=2 * CHUNK * width * half, bytes_accessed=width * half * 2, transcendentals=0
+            ),
+            name="project",
+        )(place, attended[c], out_weight)
+        mixed.append((own.astype(F32) + received[c].astype(F32)).astype(BF16))
+    return jnp.concatenate(mixed, axis=0)
+
+
+def fits_fast(mesh, queries):
+    seq, head = mesh.shape["seq"], mesh.shape["head"]
+    tokens = queries.shape[0] // seq
+    heads = queries.shape[1] // HEAD_DIM // head
+    return (
+        head == 2
+        and heads == 2 * GROUP
+        and seq == 2 * GROUP
+        and tokens % CHUNK == 0
+        and SEG1 == 2 * tokens
+        and SEG2 == GROUP * tokens
+    )
 
 
 def passed_along(value, axis, steps):
@@ -172,6 +622,10 @@
 
 def solution(mesh):
     placed = (P("seq", "head"), P("seq", "head"), P("seq", "head"), P("head", None))
-    return jax.shard_map(
-        shards, mesh=mesh, in_specs=placed, out_specs=P("seq", "head"), check_vma=False
-    )
+
+    def whole(queries, keys, values, out_weight):
+        body = fast_shards if fits_fast(mesh, queries) else shards
+        mapped = jax.shard_map(body, mesh=mesh, in_specs=placed, out_specs=P("seq", "head"), check_vma=False)
+        return mapped(queries, keys, values, out_weight)
+
+    return whole

time: 1060 us -> 264 us (0.25)
  local copies, waits for them, and re-layouts: 318 us -> 0.7 us
  matrix products: 199 us -> 0 us
  other arithmetic: 173 us -> 7.61 us
  waiting for transfers between devices: 203 us -> 47.3 us
  Pallas kernels: 0 us -> 150 us
  starting transfers between devices: 133 us -> 56.9 us
  between operations: 13.9 us -> 0.35 us
  loops' own time: 11.3 us -> 0 us
    dynamic_update_slice x48 -> x0, local copies, waits for them, and re-layouts: 242 us -> none  [shards(): near_state = lax.map(near_head, jnp.arange(heads_here))]
    dot_general x37 -> x0, matrix products: 199 us -> none  [the longest x17 85.8 us: attend_block(): jnp.einsum('hqk,khd->hqd', weights.astype(jnp.bfloat16), value_rows, pref...]
    pallas_call x0 -> x13, Pallas kernels: none -> 150 us  [the longest x1 34 us: fast_shards(): pl.pallas_call(functools.partial(near_prev_kernel, chunks), grid_spec=plt...]
    reduce_sum x20 -> x0, other arithmetic: 126 us -> none  [the longest x17 107 us: attend_block(): total = jnp.sum(weights, axis=-1)]
    reduce_scatter x1 -> x0, waiting for transfers between devices: 96.2 us -> none  [shards(): lax.psum_scatter(terms.astype(jnp.bfloat16), 'head', scatter_dimension=1,...]
    ppermute x8 -> x35, starting transfers between devices: 133 us -> 56.9 us  [the longest x8 33.7 us: fast_shards(): lax.ppermute(far_blocks[d], 'seq', ahead[d])]
    ppermute x8 -> x35, waiting for transfers between devices: 106 us -> 47.3 us  [the longest x7 20.8 us: fast_shards(): lax.ppermute(kv_blocks[d], 'seq', swaps[d])]
    concatenate x6 -> x1, other arithmetic: 30 us -> 2.25 us  [fast_shards(): return jnp.concatenate(mixed, axis=0)]
  transfers between devices with their start and end apart: 11 -> 35, of which waited for: 4 -> 12; matrix products, arithmetic and copies ran while one was open for 59% -> 2% of each run, Pallas kernels for 0% -> 54%
where the time goes in v1:
time: 264 us; the launch traced here: 262 us
  Pallas kernels  150 us (57%)
  starting transfers between devices  56.9 us (22%)
  waiting for transfers between devices  47.3 us (18%)
  other arithmetic  7.61 us (3%)
    pallas_call x1, Pallas kernels, fast_shards(): pl.pallas_call(functools.partial(near_prev_kernel, chunks), grid_spec=plt...  34 us
    ppermute x8, starting transfers between devices, fast_shards(): lax.ppermute(far_blocks[d], 'seq', ahead[d])  33.7 us
    pallas_call x4, Pallas kernels, fast_shards(): pl.pallas_call(functools.partial(combine_kernel, mid_rows, c), grid_spec=...  33.5 us
    pallas_call x1, Pallas kernels, fast_shards(): pl.pallas_call(functools.partial(near_own_kernel, chunks), grid=(heads,),...  30.7 us
    pallas_call x4, Pallas kernels, fast_shards(): pl.pallas_call(project_kernel, grid_spec=pltpu.PrefetchScalarGridSpec(num...  24.7 us
    ppermute x7, waiting for transfers between devices, fast_shards(): lax.ppermute(kv_blocks[d], 'seq', swaps[d])  20.8 us
    ppermute x4, waiting for transfers between devices, fast_shards(): received.append(lax.ppermute(send, 'head', [(0, 1), (1, 0)]))  14.3 us
    pallas_call x1, Pallas kernels, fast_shards(): pl.pallas_call(functools.partial(mid_kernel, mid_rows), grid_spec=pltpu.P...  13.8 us
  transfers between devices with their start and end apart: 35, of which 12 were waited for; matrix products, arithmetic and copies ran while one was open for 2% of the time, Pallas kernels for 54%

profile of v1, /device:TPU:1, one launch (start us, length us, event | category | flops | bytes accessed | tf_op | source)
XLA Modules:
  0.0 262.4 jit_solution(15056913309696784617)
XLA Ops:
  0.0 1.3 collective-permute-start
  1.3 1.3 collective-permute-start.1
  2.7 6.7 %prep_kv.1 = (bf16[2,256,256]{2,1,0:T(8,128)(2,1)S(1)}, bf16[2,256,256]{2,1,0:T(8,128)(2,1)S(1)}, bf16[2,256,256]{2,1,0:T(8,128)(2,1)S(1)}, bf16[2,256,256]{2,1,...) custom-call(s32[3]{0:T(128)S(1)} %pad_add_fusion.place, ...), custom_call_target="tpu_custom_call" | custom-call | tf_op jit(solution)/shard_map/prep_kv/pallas_call | solution.py:307
  9.3 5.0 %collective-permute-start.16 = (bf16[2,64,256]{2,1,0:T(8,128)(2,1)S(1)}, bf16[2,64,256]{2,1,0:T(8,128)(2,1)S(1)}, u32[]{:S(2)}, u32[]{:S(2)}) collective-permute-start(bf16[2,64,256]{2,1,0:T(8,128)(2,1)S(1)} %get-tuple-element.71), channel_id=1, source_target_pairs={{0,16},{2,18},{4,20},{6,22},{8,24},{10,26},{12,28},{14,30},{1,17},... | collective-permute-start | bytes 196616 | tf_op jit(solution)/shard_map/ppermute | solution.py:322
  14.4 6.2 %collective-permute-start.17 = (bf16[2,64,256]{2,1,0:T(8,128)(2,1)S(1)}, bf16[2,64,256]{2,1,0:T(8,128)(2,1)S(1)}, u32[]{:S(2)}, u32[]{:S(2)}) collective-permute-start(bf16[2,64,256]{2,1,0:T(8,128)(2,1)S(1)} %get-tuple-element.72), channel_id=1, source_target_pairs={{0,18},{2,16},{4,22},{6,20},{8,26},{10,24},{12,30},{14,28},{1,19},... | collective-permute-start | bytes 196616 | tf_op jit(solution)/shard_map/ppermute | solution.py:322
  20.6 1.3 collective-permute-start.18
  22.0 5.4 %collective-permute-start.19 = (bf16[2,64,256]{2,1,0:T(8,128)(2,1)S(1)}, bf16[2,64,256]{2,1,0:T(8,128)(2,1)S(1)}, u32[]{:S(2)}, u32[]{:S(2)}) collective-permute-start(bf16[2,64,256]{2,1,0:T(8,128)(2,1)S(1)} %get-tuple-element.74), channel_id=1, source_target_pairs={{0,22},{2,20},{4,18},{6,16},{8,30},{10,28},{12,26},{14,24},{1,23},... | collective-permute-start | bytes 196616 | tf_op jit(solution)/shard_map/ppermute | solution.py:322
  27.4 5.6 %collective-permute-start.20 = (bf16[2,64,256]{2,1,0:T(8,128)(2,1)S(1)}, bf16[2,64,256]{2,1,0:T(8,128)(2,1)S(1)}, u32[]{:S(2)}, u32[]{:S(2)}) collective-permute-start(bf16[2,64,256]{2,1,0:T(8,128)(2,1)S(1)} %get-tuple-element.75), channel_id=1, source_target_pairs={{0,24},{2,26},{4,28},{6,30},{8,16},{10,18},{12,20},{14,22},{1,25},... | collective-permute-start | bytes 196616 | tf_op jit(solution)/shard_map/ppermute | solution.py:322
  33.0 3.0 %collective-permute-start.21 = (bf16[2,64,256]{2,1,0:T(8,128)(2,1)S(1)}, bf16[2,64,256]{2,1,0:T(8,128)(2,1)S(1)}, u32[]{:S(2)}, u32[]{:S(2)}) collective-permute-start(bf16[2,64,256]{2,1,0:T(8,128)(2,1)S(1)} %get-tuple-element.76), channel_id=1, source_target_pairs={{0,26},{2,24},{4,30},{6,28},{8,18},{10,16},{12,22},{14,20},{1,27},... | collective-permute-start | bytes 196616 | tf_op jit(solution)/shard_map/ppermute | solution.py:322
  36.0 1.5 collective-permute-start.22
  37.5 5.6 %collective-permute-start.23 = (bf16[2,64,256]{2,1,0:T(8,128)(2,1)S(1)}, bf16[2,64,256]{2,1,0:T(8,128)(2,1)S(1)}, u32[]{:S(2)}, u32[]{:S(2)}) collective-permute-start(bf16[2,64,256]{2,1,0:T(8,128)(2,1)S(1)} %get-tuple-element.78), channel_id=1, source_target_pairs={{0,30},{2,28},{4,26},{6,24},{8,22},{10,20},{12,18},{14,16},{1,31},... | collective-permute-start | bytes 196616 | tf_op jit(solution)/shard_map/ppermute | solution.py:322
  43.1 6.2 %prep_q.1 = (bf16[1024,2048]{1,0:T(8,128)(2,1)}, bf16[256,256]{1,0:T(8,128)(2,1)S(1)}, bf16[256,256]{1,0:T(8,128)(2,1)S(1)}, bf16[256,256]{1,0:T(8,128)(2,1)S(1)...) custom-call(s32[3]{0:T(128)S(1)} %pad_add_fusion.place, ...), custom_call_target="tpu_custom_call" | custom-call | tf_op jit(solution)/shard_map/prep_q/pallas_call | solution.py:324
  49.4 2.1 collective-permute-start.11
  51.5 2.5 collective-permute-done.10.refs_10_
  54.0 3.4 %collective-permute-done.11.refs_11_ = bf16[256,256]{1,0:T(8,128)(2,1)S(1)} collective-permute-done((bf16[256,256]{1,0:T(8,128)(2,1)S(1)}, bf16[256,256]{1,0:T(8,128)(2,1)S(1)}, u32[]{:S(2)}, u32[]{:S(2)}) %collective-permute-start.11) | collective-permute-done | bytes 131104 | tf_op jit(solution)/shard_map/ppermute | solution.py:337
  57.4 1.0 collective-permute-done.13.refs_13_
  58.4 2.1 collective-permute-start.15
  60.5 2.4 collective-permute-done.14.refs_14_
  63.5 2.9 %collective-permute-done.15.refs_15_ = bf16[256,256]{1,0:T(8,128)(2,1)S(1)} collective-permute-done((bf16[256,256]{1,0:T(8,128)(2,1)S(1)}, bf16[256,256]{1,0:T(8,128)(2,1)S(1)}, u32[]{:S(2)}, u32[]{:S(2)}) %collective-permute-start.15) | collective-permute-done | bytes 131104 | tf_op jit(solution)/shard_map/ppermute | solution.py:337
  66.4 1.0 collective-permute-start.4
  67.4 4.1 %collective-permute-done.3.refs_2_ = bf16[2,256,256]{2,1,0:T(8,128)(2,1)S(1)} collective-permute-done((bf16[2,256,256]{2,1,0:T(8,128)(2,1)S(1)}, bf16[2,256,256]{2,1,0:T(8,128)(2,1)S(1)}, u32[]{:S(2)}, u32[]{:S(2)}) %collective-permute-start.3) | collective-permute-done | bytes 262176 | tf_op jit(solution)/shard_map/ppermute | solution.py:321
  71.4 3.0 %collective-permute-start.6 = (bf16[2,256,256]{2,1,0:T(8,128)(2,1)S(1)}, bf16[2,256,256]{2,1,0:T(8,128)(2,1)S(1)}, u32[]{:S(2)}, u32[]{:S(2)}) collective-permute-start(bf16[2,256,256]{2,1,0:T(8,128)(2,1)S(1)} %get-tuple-element.60), channel_id=1, source_target_pairs={{0,10},{2,8},{4,14},{6,12},{8,2},{10,0},{12,6},{14,4},{16,26},{18,... | collective-permute-start | bytes 786440 | tf_op jit(solution)/shard_map/ppermute | solution.py:321
  74.4 3.5 %collective-permute-done.4.refs_3_ = bf16[2,256,256]{2,1,0:T(8,128)(2,1)S(1)} collective-permute-done((bf16[2,256,256]{2,1,0:T(8,128)(2,1)S(1)}, bf16[2,256,256]{2,1,0:T(8,128)(2,1)S(1)}, u32[]{:S(2)}, u32[]{:S(2)}) %collective-permute-start.4) | collective-permute-done | bytes 262176 | tf_op jit(solution)/shard_map/ppermute | solution.py:321
  78.2 1.8 collective-permute-start.8
  80.0 1.5 collective-permute-done.6.refs_5_
  81.5 6.1 %collective-permute-done.7.refs_6_ = bf16[2,256,256]{2,1,0:T(8,128)(2,1)S(1)} collective-permute-done((bf16[2,256,256]{2,1,0:T(8,128)(2,1)S(1)}, bf16[2,256,256]{2,1,0:T(8,128)(2,1)S(1)}, u32[]{:S(2)}, u32[]{:S(2)}) %collective-permute-start.7) | collective-permute-done | bytes 262176 | tf_op jit(solution)/shard_map/ppermute | solution.py:321
  87.6 5.6 %collective-permute-done.8.refs_7_ = bf16[2,256,256]{2,1,0:T(8,128)(2,1)S(1)} collective-permute-done((bf16[2,256,256]{2,1,0:T(8,128)(2,1)S(1)}, bf16[2,256,256]{2,1,0:T(8,128)(2,1)S(1)}, u32[]{:S(2)}, u32[]{:S(2)}) %collective-permute-start.8) | collective-permute-done | bytes 262176 | tf_op jit(solution)/shard_map/ppermute | solution.py:321
  93.9 13.8 %mid.1 = (bf16[272,256]{1,0:T(8,128)(2,1)S(1)}, bf16[272,256]{1,0:T(8,128)(2,1)S(1)}, bf16[272,256]{1,0:T(8,128)(2,1)S(1)}, bf16[272,256]{1,0:T(8,128)(2,1)S(1)}...) custom-call(s32[3]{0:T(128)S(1)} %pad_add_fusion.place, ...), custom_call_target="tpu_custom_call" | custom-call | flops 2147483648 | bytes 4194304 | tf_op jit(solution)/shard_map/mid/pallas_call | solution.py:371
  109.1 30.7 %near_own.1 = (bf16[1024,2048]{1,0:T(8,128)(2,1)}, f32[1024,128]{1,0:T(8,128)S(1)}) custom-call(bf16[1024,2048]{1,0:T(8,128)(2,1)} %get-tuple-element.50.q_ref, bf16[1024,2048]{1,0:T(8,128)(2,1)} %k_ref.3, bf16[1024,2048]{1,0:T(8,128)(2,1)} %v_ref.3), custom_call_target="tpu_custom_call" | custom-call | flops 4294967296 | bytes 16777216 | tf_op jit(solution)/shard_map/near_own/pallas_call | solution.py:341
  140.8 1.7 collective-permute-start.28
  143.4 1.7 collective-permute-start.30
  145.1 34.0 %near_prev.1 = (bf16[1024,2048]{1,0:T(8,128)(2,1)}, f32[1024,128]{1,0:T(8,128)S(1)}) custom-call(s32[3]{0:T(128)S(1)} %pad_add_fusion.place, bf16[1024,2048]{1,0:T(8,128)(2,1)} %get-tuple-element.50.q_ref, bf16[1024,2048]{1,0:T(8,128)(2,1)} %collective-permute-done.k_ref, bf16[1024,2048]{1,0:T(8,128)(2,1)} %collective-permute-done.1.v_ref, ...), custom_call_target="tpu_custom_call" | custom-call | flops 8589934592 | bytes 16777216 | tf_op jit(solution)/shard_map/near_prev/pallas_call | solution.py:353
  179.1 8.4 %combine.7 = (bf16[256,2048]{1,0:T(8,128)(2,1)S(1)}, bf16[256,2048]{1,0:T(8,128)(2,1)S(1)}) custom-call(s32[3]{0:T(128)S(1)} %pad_add_fusion.place, bf16[1024,2048]{1,0:T(8,128)(2,1)} %get-tuple-element.53.o_ref, f32[1024,128]{1,0:T(8,128)S(1)} %get-tuple-element.54.lse_ref, bf16[272,256]{1,0:T(8,128)(2,1)S(1)} %get-tuple-element.79.refs_0_, ...), custom_call_target="tpu_custom_call" | custom-call | flops 2147483648 | bytes 8388608 | tf_op jit(solution)/shard_map/combine/pallas_call | solution.py:402
  187.5 1.3 collective-permute-start.34
  188.8 8.4 %combine.6 = (bf16[256,2048]{1,0:T(8,128)(2,1)S(1)}, bf16[256,2048]{1,0:T(8,128)(2,1)S(1)}) custom-call(s32[3]{0:T(128)S(1)} %pad_add_fusion.place, bf16[1024,2048]{1,0:T(8,128)(2,1)} %get-tuple-element.53.o_ref, f32[1024,128]{1,0:T(8,128)S(1)} %get-tuple-element.54.lse_ref, bf16[272,256]{1,0:T(8,128)(2,1)S(1)} %get-tuple-element.79.refs_0_, ...), custom_call_target="tpu_custom_call" | custom-call | flops 2147483648 | bytes 8388608 | tf_op jit(solution)/shard_map/combine/pallas_call | solution.py:402
  197.5 8.4 %combine.5 = (bf16[256,2048]{1,0:T(8,128)(2,1)S(1)}, bf16[256,2048]{1,0:T(8,128)(2,1)S(1)}) custom-call(s32[3]{0:T(128)S(1)} %pad_add_fusion.place, bf16[1024,2048]{1,0:T(8,128)(2,1)} %get-tuple-element.53.o_ref, f32[1024,128]{1,0:T(8,128)S(1)} %get-tuple-element.54.lse_ref, bf16[272,256]{1,0:T(8,128)(2,1)S(1)} %get-tuple-element.79.refs_0_, ...), custom_call_target="tpu_custom_call" | custom-call | flops 2147483648 | bytes 8388608 | tf_op jit(solution)/shard_map/combine/pallas_call | solution.py:402
  205.9 1.3 collective-permute-start.32
  207.2 8.4 %combine.4 = (bf16[256,2048]{1,0:T(8,128)(2,1)S(1)}, bf16[256,2048]{1,0:T(8,128)(2,1)S(1)}) custom-call(s32[3]{0:T(128)S(1)} %pad_add_fusion.place, bf16[1024,2048]{1,0:T(8,128)(2,1)} %get-tuple-element.53.o_ref, f32[1024,128]{1,0:T(8,128)S(1)} %get-tuple-element.54.lse_ref, bf16[272,256]{1,0:T(8,128)(2,1)S(1)} %get-tuple-element.79.refs_0_, ...), custom_call_target="tpu_custom_call" | custom-call | flops 2147483648 | bytes 8388608 | tf_op jit(solution)/shard_map/combine/pallas_call | solution.py:402
  215.8 6.1 %project.7 = bf16[256,2048]{1,0:T(8,128)(2,1)S(1)} custom-call(s32[3]{0:T(128)S(1)} %pad_add_fusion.place, bf16[256,2048]{1,0:T(8,128)(2,1)S(1)} %get-tuple-element.93.att_ref, bf16[2048,4096]{1,0:T(8,128)(2,1)} %w_ref.7), custom_call_target="tpu_custom_call" | custom-call | flops 2147483648 | bytes 8388608 | tf_op jit(solution)/shard_map/project/pallas_call | solution.py:430
  221.9 6.3 %project.6 = bf16[256,2048]{1,0:T(8,128)(2,1)S(1)} custom-call(s32[3]{0:T(128)S(1)} %pad_add_fusion.place, bf16[256,2048]{1,0:T(8,128)(2,1)S(1)} %get-tuple-element.91.att_ref, bf16[2048,4096]{1,0:T(8,128)(2,1)} %w_ref.7), custom_call_target="tpu_custom_call" | custom-call | flops 2147483648 | bytes 8388608 | tf_op jit(solution)/shard_map/project/pallas_call | solution.py:430
  228.3 6.1 %project.5 = bf16[256,2048]{1,0:T(8,128)(2,1)S(1)} custom-call(s32[3]{0:T(128)S(1)} %pad_add_fusion.place, bf16[256,2048]{1,0:T(8,128)(2,1)S(1)} %get-tuple-element.89.att_ref, bf16[2048,4096]{1,0:T(8,128)(2,1)} %w_ref.7), custom_call_target="tpu_custom_call" | custom-call | flops 2147483648 | bytes 8388608 | tf_op jit(solution)/shard_map/project/pallas_call | solution.py:430
  234.4 6.1 %project.4 = bf16[256,2048]{1,0:T(8,128)(2,1)S(1)} custom-call(s32[3]{0:T(128)S(1)} %pad_add_fusion.place, bf16[256,2048]{1,0:T(8,128)(2,1)S(1)} %get-tuple-element.87.att_ref, bf16[2048,4096]{1,0:T(8,128)(2,1)} %w_ref.7), custom_call_target="tpu_custom_call" | custom-call | flops 2147483648 | bytes 8388608 | tf_op jit(solution)/shard_map/project/pallas_call | solution.py:430
  240.6 1.6 add_convert_fusion
  242.2 1.6 add_convert_fusion.1
  243.8 4.8 %collective-permute-done.32 = bf16[256,2048]{1,0:T(8,128)(2,1)} collective-permute-done((bf16[256,2048]{1,0:T(8,128)(2,1)S(1)}, bf16[256,2048]{1,0:T(8,128)(2,1)}, u32[]{:S(2)}, u32[]{:S(2)}) %collective-permute-start.32) | collective-permute-done | bytes 1048608 | tf_op jit(solution)/shard_map/ppermute | solution.py:426
  248.6 1.6 add_convert_fusion.2
  250.2 9.5 %collective-permute-done.31 = bf16[256,2048]{1,0:T(8,128)(2,1)S(1)} collective-permute-done((bf16[256,2048]{1,0:T(8,128)(2,1)S(1)}, bf16[256,2048]{1,0:T(8,128)(2,1)S(1)}, u32[]{:S(2)}, u32[]{:S(2)}) %collective-permute-start.31) | collective-permute-done | bytes 1048608 | tf_op jit(solution)/shard_map/ppermute | solution.py:426
  260.1 2.2 pad_maximum_fusion
  (47 shorter events, 6.1 us)
Async XLA Ops:
  0.0 142.5 %collective-permute-start = (bf16[1024,2048]{1,0:T(8,128)(2,1)}, bf16[1024,2048]{1,0:T(8,128)(2,1)}, u32[]{:S(2)}, u32[]{:S(2)}) collective-permute-start(bf16[1024,2048]{1,0:T(8,128)(2,1)} %k_ref.3), channel_id=1, source_target_pairs={{0,2},{4,6},{8,10},{12,14},{16,18},{20,22},{24,26},{28,30},{1,3},{... | collective-permute-start | bytes 12582920 | tf_op jit(solution)/shard_map/ppermute | solution.py:304
  1.3 142.1 %collective-permute-start.1 = (bf16[1024,2048]{1,0:T(8,128)(2,1)}, bf16[1024,2048]{1,0:T(8,128)(2,1)}, u32[]{:S(2)}, u32[]{:S(2)}) collective-permute-start(bf16[1024,2048]{1,0:T(8,128)(2,1)} %v_ref.3), channel_id=1, source_target_pairs={{0,2},{4,6},{8,10},{12,14},{16,18},{20,22},{24,26},{28,30},{1,3},{... | collective-permute-start | bytes 12582920 | tf_op jit(solution)/shard_map/ppermute | solution.py:305
  9.3 12.6 %collective-permute-start.16 = (bf16[2,64,256]{2,1,0:T(8,128)(2,1)S(1)}, bf16[2,64,256]{2,1,0:T(8,128)(2,1)S(1)}, u32[]{:S(2)}, u32[]{:S(2)}) collective-permute-start(bf16[2,64,256]{2,1,0:T(8,128)(2,1)S(1)} %get-tuple-element.71), channel_id=1, source_target_pairs={{0,16},{2,18},{4,20},{6,22},{8,24},{10,26},{12,28},{14,30},{1,17},... | collective-permute-start | bytes 196616 | tf_op jit(solution)/shard_map/ppermute | solution.py:322
  14.4 13.0 %collective-permute-start.17 = (bf16[2,64,256]{2,1,0:T(8,128)(2,1)S(1)}, bf16[2,64,256]{2,1,0:T(8,128)(2,1)S(1)}, u32[]{:S(2)}, u32[]{:S(2)}) collective-permute-start(bf16[2,64,256]{2,1,0:T(8,128)(2,1)S(1)} %get-tuple-element.72), channel_id=1, source_target_pairs={{0,18},{2,16},{4,22},{6,20},{8,26},{10,24},{12,30},{14,28},{1,19},... | collective-permute-start | bytes 196616 | tf_op jit(solution)/shard_map/ppermute | solution.py:322
  20.6 12.3 %collective-permute-start.18 = (bf16[2,64,256]{2,1,0:T(8,128)(2,1)S(1)}, bf16[2,64,256]{2,1,0:T(8,128)(2,1)S(1)}, u32[]{:S(2)}, u32[]{:S(2)}) collective-permute-start(bf16[2,64,256]{2,1,0:T(8,128)(2,1)S(1)} %get-tuple-element.73), channel_id=1, source_target_pairs={{0,20},{2,22},{4,16},{6,18},{8,28},{10,30},{12,24},{14,26},{1,21},... | collective-permute-start | bytes 196616 | tf_op jit(solution)/shard_map/ppermute | solution.py:322
  22.0 14.0 %collective-permute-start.19 = (bf16[2,64,256]{2,1,0:T(8,128)(2,1)S(1)}, bf16[2,64,256]{2,1,0:T(8,128)(2,1)S(1)}, u32[]{:S(2)}, u32[]{:S(2)}) collective-permute-start(bf16[2,64,256]{2,1,0:T(8,128)(2,1)S(1)} %get-tuple-element.74), channel_id=1, source_target_pairs={{0,22},{2,20},{4,18},{6,16},{8,30},{10,28},{12,26},{14,24},{1,23},... | collective-permute-start | bytes 196616 | tf_op jit(solution)/shard_map/ppermute | solution.py:322
  27.4 10.1 %collective-permute-start.20 = (bf16[2,64,256]{2,1,0:T(8,128)(2,1)S(1)}, bf16[2,64,256]{2,1,0:T(8,128)(2,1)S(1)}, u32[]{:S(2)}, u32[]{:S(2)}) collective-permute-start(bf16[2,64,256]{2,1,0:T(8,128)(2,1)S(1)} %get-tuple-element.75), channel_id=1, source_target_pairs={{0,24},{2,26},{4,28},{6,30},{8,16},{10,18},{12,20},{14,22},{1,25},... | collective-permute-start | bytes 196616 | tf_op jit(solution)/shard_map/ppermute | solution.py:322
  33.0 16.3 %collective-permute-start.21 = (bf16[2,64,256]{2,1,0:T(8,128)(2,1)S(1)}, bf16[2,64,256]{2,1,0:T(8,128)(2,1)S(1)}, u32[]{:S(2)}, u32[]{:S(2)}) collective-permute-start(bf16[2,64,256]{2,1,0:T(8,128)(2,1)S(1)} %get-tuple-element.76), channel_id=1, source_target_pairs={{0,26},{2,24},{4,30},{6,28},{8,18},{10,16},{12,22},{14,20},{1,27},... | collective-permute-start | bytes 196616 | tf_op jit(solution)/shard_map/ppermute | solution.py:322
  36.0 13.3 %collective-permute-start.22 = (bf16[2,64,256]{2,1,0:T(8,128)(2,1)S(1)}, bf16[2,64,256]{2,1,0:T(8,128)(2,1)S(1)}, u32[]{:S(2)}, u32[]{:S(2)}) collective-permute-start(bf16[2,64,256]{2,1,0:T(8,128)(2,1)S(1)} %get-tuple-element.77), channel_id=1, source_target_pairs={{0,28},{2,30},{4,24},{6,26},{8,20},{10,22},{12,16},{14,18},{1,29},... | collective-permute-start | bytes 196616 | tf_op jit(solution)/shard_map/ppermute | solution.py:322
  37.5 11.9 %collective-permute-start.23 = (bf16[2,64,256]{2,1,0:T(8,128)(2,1)S(1)}, bf16[2,64,256]{2,1,0:T(8,128)(2,1)S(1)}, u32[]{:S(2)}, u32[]{:S(2)}) collective-permute-start(bf16[2,64,256]{2,1,0:T(8,128)(2,1)S(1)} %get-tuple-element.78), channel_id=1, source_target_pairs={{0,30},{2,28},{4,26},{6,24},{8,22},{10,20},{12,18},{14,16},{1,31},... | collective-permute-start | bytes 196616 | tf_op jit(solution)/shard_map/ppermute | solution.py:322
  49.3 2.2 collective-permute-start.9
  49.3 4.7 %collective-permute-start.10 = (bf16[256,256]{1,0:T(8,128)(2,1)S(1)}, bf16[256,256]{1,0:T(8,128)(2,1)S(1)}, u32[]{:S(2)}, u32[]{:S(2)}) collective-permute-start(bf16[256,256]{1,0:T(8,128)(2,1)S(1)} %get-tuple-element.65), channel_id=1, source_target_pairs={{0,4},{2,6},{4,0},{6,2},{8,12},{10,14},{12,8},{14,10},{16,20},{18,... | collective-permute-start | bytes 393224 | tf_op jit(solution)/shard_map/ppermute | solution.py:337
  49.4 8.0 %collective-permute-start.11 = (bf16[256,256]{1,0:T(8,128)(2,1)S(1)}, bf16[256,256]{1,0:T(8,128)(2,1)S(1)}, u32[]{:S(2)}, u32[]{:S(2)}) collective-permute-start(bf16[256,256]{1,0:T(8,128)(2,1)S(1)} %get-tuple-element.66), channel_id=1, source_target_pairs={{0,6},{2,4},{4,2},{6,0},{8,14},{10,12},{12,10},{14,8},{16,22},{18,... | collective-permute-start | bytes 393224 | tf_op jit(solution)/shard_map/ppermute | solution.py:337
  51.5 6.0 %collective-permute-start.12 = (bf16[256,256]{1,0:T(8,128)(2,1)S(1)}, bf16[256,256]{1,0:T(8,128)(2,1)S(1)}, u32[]{:S(2)}, u32[]{:S(2)}) collective-permute-start(bf16[256,256]{1,0:T(8,128)(2,1)S(1)} %get-tuple-element.67), channel_id=1, source_target_pairs={{0,8},{2,10},{4,12},{6,14},{8,0},{10,2},{12,4},{14,6},{16,24},{18,... | collective-permute-start | bytes 393224 | tf_op jit(solution)/shard_map/ppermute | solution.py:337
  54.0 4.4 %collective-permute-start.13 = (bf16[256,256]{1,0:T(8,128)(2,1)S(1)}, bf16[256,256]{1,0:T(8,128)(2,1)S(1)}, u32[]{:S(2)}, u32[]{:S(2)}) collective-permute-start(bf16[256,256]{1,0:T(8,128)(2,1)S(1)} %get-tuple-element.68), channel_id=1, source_target_pairs={{0,10},{2,8},{4,14},{6,12},{8,2},{10,0},{12,6},{14,4},{16,26},{18,... | collective-permute-start | bytes 393224 | tf_op jit(solution)/shard_map/ppermute | solution.py:337
  57.4 9.9 %collective-permute-start.2 = (bf16[2,256,256]{2,1,0:T(8,128)(2,1)S(1)}, bf16[2,256,256]{2,1,0:T(8,128)(2,1)S(1)}, u32[]{:S(2)}, u32[]{:S(2)}) collective-permute-start(bf16[2,256,256]{2,1,0:T(8,128)(2,1)S(1)} %get-tuple-element.56), channel_id=1, source_target_pairs={{0,2},{2,0},{4,6},{6,4},{8,10},{10,8},{12,14},{14,12},{16,18},{18,... | collective-permute-start | bytes 786440 | tf_op jit(solution)/shard_map/ppermute | solution.py:321
  57.4 5.5 %collective-permute-start.14 = (bf16[256,256]{1,0:T(8,128)(2,1)S(1)}, bf16[256,256]{1,0:T(8,128)(2,1)S(1)}, u32[]{:S(2)}, u32[]{:S(2)}) collective-permute-start(bf16[256,256]{1,0:T(8,128)(2,1)S(1)} %get-tuple-element.69), channel_id=1, source_target_pairs={{0,12},{2,14},{4,8},{6,10},{8,4},{10,6},{12,0},{14,2},{16,28},{18,... | collective-permute-start | bytes 393224 | tf_op jit(solution)/shard_map/ppermute | solution.py:337
  58.4 7.9 %collective-permute-start.15 = (bf16[256,256]{1,0:T(8,128)(2,1)S(1)}, bf16[256,256]{1,0:T(8,128)(2,1)S(1)}, u32[]{:S(2)}, u32[]{:S(2)}) collective-permute-start(bf16[256,256]{1,0:T(8,128)(2,1)S(1)} %get-tuple-element.70), channel_id=1, source_target_pairs={{0,14},{2,12},{4,10},{6,8},{8,6},{10,4},{12,2},{14,0},{16,30},{18,... | collective-permute-start | bytes 393224 | tf_op jit(solution)/shard_map/ppermute | solution.py:337
  62.9 8.6 %collective-permute-start.3 = (bf16[2,256,256]{2,1,0:T(8,128)(2,1)S(1)}, bf16[2,256,256]{2,1,0:T(8,128)(2,1)S(1)}, u32[]{:S(2)}, u32[]{:S(2)}) collective-permute-start(bf16[2,256,256]{2,1,0:T(8,128)(2,1)S(1)} %get-tuple-element.57), channel_id=1, source_target_pairs={{0,4},{2,6},{4,0},{6,2},{8,12},{10,14},{12,8},{14,10},{16,20},{18,... | collective-permute-start | bytes 786440 | tf_op jit(solution)/shard_map/ppermute | solution.py:321
  66.4 11.5 %collective-permute-start.4 = (bf16[2,256,256]{2,1,0:T(8,128)(2,1)S(1)}, bf16[2,256,256]{2,1,0:T(8,128)(2,1)S(1)}, u32[]{:S(2)}, u32[]{:S(2)}) collective-permute-start(bf16[2,256,256]{2,1,0:T(8,128)(2,1)S(1)} %get-tuple-element.58), channel_id=1, source_target_pairs={{0,6},{2,4},{4,2},{6,0},{8,14},{10,12},{12,10},{14,8},{16,22},{18,... | collective-permute-start | bytes 786440 | tf_op jit(solution)/shard_map/ppermute | solution.py:321
  67.4 10.9 %collective-permute-start.5 = (bf16[2,256,256]{2,1,0:T(8,128)(2,1)S(1)}, bf16[2,256,256]{2,1,0:T(8,128)(2,1)S(1)}, u32[]{:S(2)}, u32[]{:S(2)}) collective-permute-start(bf16[2,256,256]{2,1,0:T(8,128)(2,1)S(1)} %get-tuple-element.59), channel_id=1, source_target_pairs={{0,8},{2,10},{4,12},{6,14},{8,0},{10,2},{12,4},{14,6},{16,24},{18,... | collective-permute-start | bytes 786440 | tf_op jit(solution)/shard_map/ppermute | solution.py:321
  71.4 10.0 %collective-permute-start.6 = (bf16[2,256,256]{2,1,0:T(8,128)(2,1)S(1)}, bf16[2,256,256]{2,1,0:T(8,128)(2,1)S(1)}, u32[]{:S(2)}, u32[]{:S(2)}) collective-permute-start(bf16[2,256,256]{2,1,0:T(8,128)(2,1)S(1)} %get-tuple-element.60), channel_id=1, source_target_pairs={{0,10},{2,8},{4,14},{6,12},{8,2},{10,0},{12,6},{14,4},{16,26},{18,... | collective-permute-start | bytes 786440 | tf_op jit(solution)/shard_map/ppermute | solution.py:321
  77.9 9.7 %collective-permute-start.7 = (bf16[2,256,256]{2,1,0:T(8,128)(2,1)S(1)}, bf16[2,256,256]{2,1,0:T(8,128)(2,1)S(1)}, u32[]{:S(2)}, u32[]{:S(2)}) collective-permute-start(bf16[2,256,256]{2,1,0:T(8,128)(2,1)S(1)} %get-tuple-element.61), channel_id=1, source_target_pairs={{0,12},{2,14},{4,8},{6,10},{8,4},{10,6},{12,0},{14,2},{16,28},{18,... | collective-permute-start | bytes 786440 | tf_op jit(solution)/shard_map/ppermute | solution.py:321
  78.2 15.0 %collective-permute-start.8 = (bf16[2,256,256]{2,1,0:T(8,128)(2,1)S(1)}, bf16[2,256,256]{2,1,0:T(8,128)(2,1)S(1)}, u32[]{:S(2)}, u32[]{:S(2)}) collective-permute-start(bf16[2,256,256]{2,1,0:T(8,128)(2,1)S(1)} %get-tuple-element.62), channel_id=1, source_target_pairs={{0,14},{2,12},{4,10},{6,8},{8,6},{10,4},{12,2},{14,0},{16,30},{18,... | collective-permute-start | bytes 786440 | tf_op jit(solution)/shard_map/ppermute | solution.py:321
  81.5 11.7 %copy-start = (bf16[2,256,256]{2,1,0:T(8,128)(2,1)}, bf16[2,256,256]{2,1,0:T(8,128)(2,1)S(1)}, u32[]{:S(2)}) copy-start(bf16[2,256,256]{2,1,0:T(8,128)(2,1)S(1)} %collective-permute-done.6.refs_5_) | copy-start | bytes 786436
  87.6 5.6 %copy-start.1 = (bf16[2,256,256]{2,1,0:T(8,128)(2,1)}, bf16[2,256,256]{2,1,0:T(8,128)(2,1)S(1)}, u32[]{:S(2)}) copy-start(bf16[2,256,256]{2,1,0:T(8,128)(2,1)S(1)} %collective-permute-done.7.refs_6_) | copy-start | bytes 786436
  93.2 0.7 copy-start.2
  107.8 32.9 %collective-permute-start.24 = (bf16[272,256]{1,0:T(8,128)(2,1)S(1)}, bf16[272,256]{1,0:T(8,128)(2,1)S(1)}, u32[]{:S(2)}, u32[]{:S(2)}) collective-permute-start(bf16[272,256]{1,0:T(8,128)(2,1)S(1)} %get-tuple-element.80), channel_id=1, source_target_pairs={{0,2},{2,0},{4,6},{6,4},{8,10},{10,8},{12,14},{14,12},{16,18},{18,... | collective-permute-start | bytes 417800 | tf_op jit(solution)/shard_map/ppermute | solution.py:394
  108.2 32.6 %collective-permute-start.25 = (bf16[272,256]{1,0:T(8,128)(2,1)S(1)}, bf16[272,256]{1,0:T(8,128)(2,1)S(1)}, u32[]{:S(2)}, u32[]{:S(2)}) collective-permute-start(bf16[272,256]{1,0:T(8,128)(2,1)S(1)} %get-tuple-element.81), channel_id=1, source_target_pairs={{0,4},{2,6},{4,0},{6,2},{8,12},{10,14},{12,8},{14,10},{16,20},{18,... | collective-permute-start | bytes 417800 | tf_op jit(solution)/shard_map/ppermute | solution.py:394
  139.8 39.3 %collective-permute-start.26 = (bf16[272,256]{1,0:T(8,128)(2,1)S(1)}, bf16[272,256]{1,0:T(8,128)(2,1)S(1)}, u32[]{:S(2)}, u32[]{:S(2)}) collective-permute-start(bf16[272,256]{1,0:T(8,128)(2,1)S(1)} %get-tuple-element.82), channel_id=1, source_target_pairs={{0,6},{2,4},{4,2},{6,0},{8,14},{10,12},{12,10},{14,8},{16,22},{18,... | collective-permute-start | bytes 417800 | tf_op jit(solution)/shard_map/ppermute | solution.py:394
  140.7 38.4 %collective-permute-start.27 = (bf16[272,256]{1,0:T(8,128)(2,1)S(1)}, bf16[272,256]{1,0:T(8,128)(2,1)S(1)}, u32[]{:S(2)}, u32[]{:S(2)}) collective-permute-start(bf16[272,256]{1,0:T(8,128)(2,1)S(1)} %get-tuple-element.83), channel_id=1, source_target_pairs={{0,8},{2,10},{4,12},{6,14},{8,0},{10,2},{12,4},{14,6},{16,24},{18,... | collective-permute-start | bytes 417800 | tf_op jit(solution)/shard_map/ppermute | solution.py:394
  140.8 38.2 %collective-permute-start.28 = (bf16[272,256]{1,0:T(8,128)(2,1)S(1)}, bf16[272,256]{1,0:T(8,128)(2,1)S(1)}, u32[]{:S(2)}, u32[]{:S(2)}) collective-permute-start(bf16[272,256]{1,0:T(8,128)(2,1)S(1)} %get-tuple-element.84), channel_id=1, source_target_pairs={{0,10},{2,8},{4,14},{6,12},{8,2},{10,0},{12,6},{14,4},{16,26},{18,... | collective-permute-start | bytes 417800 | tf_op jit(solution)/shard_map/ppermute | solution.py:394
  142.5 36.6 %collective-permute-start.29 = (bf16[272,256]{1,0:T(8,128)(2,1)S(1)}, bf16[272,256]{1,0:T(8,128)(2,1)S(1)}, u32[]{:S(2)}, u32[]{:S(2)}) collective-permute-start(bf16[272,256]{1,0:T(8,128)(2,1)S(1)} %get-tuple-element.85), channel_id=1, source_target_pairs={{0,12},{2,14},{4,8},{6,10},{8,4},{10,6},{12,0},{14,2},{16,28},{18,... | collective-permute-start | bytes 417800 | tf_op jit(solution)/shard_map/ppermute | solution.py:394
  143.4 35.7 %collective-permute-start.30 = (bf16[272,256]{1,0:T(8,128)(2,1)S(1)}, bf16[272,256]{1,0:T(8,128)(2,1)S(1)}, u32[]{:S(2)}, u32[]{:S(2)}) collective-permute-start(bf16[272,256]{1,0:T(8,128)(2,1)S(1)} %get-tuple-element.86), channel_id=1, source_target_pairs={{0,14},{2,12},{4,10},{6,8},{8,6},{10,4},{12,2},{14,0},{16,30},{18,... | collective-permute-start | bytes 417800 | tf_op jit(solution)/shard_map/ppermute | solution.py:394
  187.5 53.0 %collective-permute-start.34 = (bf16[256,2048]{1,0:T(8,128)(2,1)S(1)}, bf16[256,2048]{1,0:T(8,128)(2,1)}, u32[]{:S(2)}, u32[]{:S(2)}) collective-permute-start(bf16[256,2048]{1,0:T(8,128)(2,1)S(1)} %get-tuple-element.94), channel_id=1, source_target_pairs={{0,1},{1,0},{2,3},{3,2},{4,5},{5,4},{6,7},{7,6},{8,9},{9,8},{10,11... | collective-permute-start | bytes 3145736 | tf_op jit(solution)/shard_map/ppermute | solution.py:426
  197.2 45.0 %collective-permute-start.33 = (bf16[256,2048]{1,0:T(8,128)(2,1)S(1)}, bf16[256,2048]{1,0:T(8,128)(2,1)}, u32[]{:S(2)}, u32[]{:S(2)}) collective-permute-start(bf16[256,2048]{1,0:T(8,128)(2,1)S(1)} %get-tuple-element.92), channel_id=1, source_target_pairs={{0,1},{1,0},{2,3},{3,2},{4,5},{5,4},{6,7},{7,6},{8,9},{9,8},{10,11... | collective-permute-start | bytes 3145736 | tf_op jit(solution)/shard_map/ppermute | solution.py:426
  205.9 42.7 %collective-permute-start.32 = (bf16[256,2048]{1,0:T(8,128)(2,1)S(1)}, bf16[256,2048]{1,0:T(8,128)(2,1)}, u32[]{:S(2)}, u32[]{:S(2)}) collective-permute-start(bf16[256,2048]{1,0:T(8,128)(2,1)S(1)} %get-tuple-element.90), channel_id=1, source_target_pairs={{0,1},{1,0},{2,3},{3,2},{4,5},{5,4},{6,7},{7,6},{8,9},{9,8},{10,11... | collective-permute-start | bytes 3145736 | tf_op jit(solution)/shard_map/ppermute | solution.py:426
  215.5 44.2 %collective-permute-start.31 = (bf16[256,2048]{1,0:T(8,128)(2,1)S(1)}, bf16[256,2048]{1,0:T(8,128)(2,1)S(1)}, u32[]{:S(2)}, u32[]{:S(2)}) collective-permute-start(bf16[256,2048]{1,0:T(8,128)(2,1)S(1)} %get-tuple-element.88), channel_id=1, source_target_pairs={{0,1},{1,0},{2,3},{3,2},{4,5},{5,4},{6,7},{7,6},{8,9},{9,8},{10,11... | collective-permute-start | bytes 3145736 | tf_op jit(solution)/shard_map/ppermute | solution.py:426
